TPU v7x, 128 devices: a whole 4x4x4 slice. The times are simulated.
128 devices in a mesh: dp: 16 (over y, z), tensor: 8 (over x, core).
Axes of the slice: x: 4, y: 4, z: 4, core: 2. Of those that a mesh axis runs over, the one named last changes fastest.
Arguments:
- grad: bfloat16 [16, 2, 3072, 5120], P('dp', None, 'tensor'), may hold values from -32 to 32
- error: bfloat16 [16, 2, 3072, 5120], P('dp', None, 'tensor'), may hold values from -4 to 4
- q_init: bfloat16 [5120, 2, 32], replicated, may hold values from -6 to 6
Outputs:
- new_error: bfloat16 [16, 2, 3072, 5120], P('dp', None, 'tensor')
- p_factor: float32 [2, 3072, 32], P(None, 'tensor')
- q_factor: float32 [5120, 2, 32], P(('dp', 'tensor'))
All inputs are finite; a program needn't handle non-finite values.
Results may differ from a plain program's by a relative error of at most 0.018.
Values may be sent and summed in bfloat16 or wider, within the bound.
No kernel may reach another device: no remote copies, remote signals or barrier semaphores. Data moves between devices by JAX's collectives and lax.ppermute only.
A program may use at most 128 MiB of HBM per device.

v0:
```python
import jax
import jax.numpy as jnp
from jax import lax
from jax.sharding import PartitionSpec as P


def inverse_factor(gram):
    rank_width = gram.shape[-1]
    identity = jnp.eye(rank_width, dtype=jnp.float32)
    trace_sum = jnp.trace(gram, axis1=1, axis2=2)
    shifted = gram + (1e-05 * trace_sum / rank_width)[:, None, None] * identity
    factor = jnp.linalg.cholesky(shifted)
    return jax.vmap(lambda single: jax.scipy.linalg.solve_triangular(single, identity, lower=True))(
        factor
    )


def compress(corrected, q_start):
    partial_p = jnp.einsum("mrd,dmk->mrk", corrected, q_start, preferred_element_type=jnp.float32)
    summed = lax.psum(partial_p.astype(jnp.bfloat16), "dp").astype(jnp.float32)
    gram_part = jnp.einsum("mrk,mrl->mkl", summed, summed, precision=lax.Precision.HIGHEST)
    gram_full = lax.psum(gram_part, "tensor")
    inverse = inverse_factor(gram_full)
    p_factor = jnp.einsum("mrk,mlk->mrl", summed, inverse, precision=lax.Precision.HIGHEST)
    p_round = summed.astype(jnp.bfloat16)
    p_factor_round = p_factor.astype(jnp.bfloat16)
    replicas = lax.axis_size("dp")
    devices = lax.axis_size(("dp", "tensor"))
    share_rows = corrected.shape[2] // devices
    projected = jnp.einsum("mrd,mrk->dmk", corrected, p_round, preferred_element_type=jnp.float32)
    total_sum = lax.psum(projected, ("dp", "tensor"))
    q_full = (
        jnp.einsum("dmk,mlk->dml", total_sum, inverse, precision=lax.Precision.HIGHEST) / replicas
    )
    q_own = lax.dynamic_slice_in_dim(
        q_full, lax.axis_index(("dp", "tensor")) * share_rows, share_rows, 0
    )
    q_round = q_full.astype(jnp.bfloat16)
    rebuilt = jnp.einsum(
        "mrk,dmk->mrd", p_factor_round, q_round, preferred_element_type=jnp.float32
    )
    new_error = (corrected.astype(jnp.float32) - rebuilt).astype(jnp.bfloat16)
    return (new_error, p_factor, q_own)


def local(grad, error, q_init):
    corrected = (grad[0].astype(jnp.float32) + error[0].astype(jnp.float32)).astype(jnp.bfloat16)
    new_error, p_factor, q_factor = compress(corrected, q_init)
    return (new_error[None], p_factor, q_factor)


def solution(mesh):
    in_specs = (P("dp", None, "tensor", None), P("dp", None, "tensor", None), P())
    out_specs = (
        P("dp", None, "tensor", None),
        P(None, "tensor", None),
        P(("dp", "tensor"), None, None),
    )
    return jax.shard_map(local, mesh=mesh, in_specs=in_specs, out_specs=out_specs, check_vma=False)
```

profile of v0, /device:TPU:1, one launch (start us, length us, event | category | flops | bytes accessed | tf_op | source)
XLA Modules:
  0.0 265.5 jit_solution(13808662391409382241)
XLA Ops:
  7.2 0.0 copy-start
  7.2 0.0 all-reduce.2.cloned.1.call-start
  7.2 1.0 copy-done
  8.3 7.9 %convolution_convert_fusion = bf16[2,384,32]{1,2,0:T(8,128)(2,1)S(1)} fusion(bf16[5120,2,32]{0,2,1:T(8,128)(2,1)S(1)} %copy-done, bf16[1,2,384,5120]{3,2,1,0:T(8,128)(2,1)} %param.4, bf16[1,2,384,5120]{3,2,1,0:T(8,128)(2,1)} %param.3), kind=kOutput, calls=%fused_computation.6 | convolution fusion | flops 267411456 | bytes 16433152 | tf_op jit(solution)/shard_map/mrd,dmk->mrk/dot_general | solution.py:19
  16.2 62.7 %psum.21 = bf16[2,384,32]{1,2,0:T(8,128)(2,1)S(1)} all-reduce(bf16[2,384,32]{1,2,0:T(8,128)(2,1)S(1)} %convolution_convert_fusion), channel_id=1, replica_groups=mesh['dp'=16,'tensor'=8] {'dp'}, use_global_device_ids=true, to_apply=%region_0.0 | all-reduce | flops 24576 | bytes 98304 | tf_op jit(solution)/shard_map/psum | solution.py:20
  78.9 8.8 %convolution_bitcast_fusion = f32[5120,2,32]{0,2,1:T(8,128)} fusion(bf16[2,384,32]{1,2,0:T(8,128)(2,1)S(1)} %psum.21, bf16[1,2,384,5120]{3,2,1,0:T(8,128)(2,1)} %param.4, bf16[1,2,384,5120]{3,2,1,0:T(8,128)(2,1)} %param.3), kind=kOutput, calls=%fused_computation.5 | convolution fusion | flops 267386880 | bytes 17088512 | tf_op jit(solution)/shard_map/mrd,mrk->dmk/dot_general | solution.py:30
  87.8 0.0 all-reduce.2.cloned.1.call-update
  87.8 0.1 fusion.12
  88.0 35.1 %psum.22 = f32[2,32,32]{2,1,0:T(8,128)S(1)} all-reduce(f32[2,32,32]{2,1,0:T(8,128)S(1)} %fusion.12), channel_id=1, replica_groups=mesh['dp'=16,'tensor'=8] {'tensor'}, use_global_device_ids=true, to_apply=%region_1.0 | all-reduce | flops 2048 | bytes 16384 | tf_op jit(solution)/shard_map/psum | solution.py:22
  123.0 0.1 select_reduce_fusion.1
  123.1 0.1 multiply_add_fusion
  123.2 0.1 copy.8
  123.3 0.1 fusion.7
  123.4 5.9 %custom-call.8 = f32[2,32,32]{2,1,0:T(8,128)S(1)} custom-call(f32[2,32,32]{2,1,0:T(8,128)S(1)} %fusion.7), custom_call_target="Cholesky" | custom-call | tf_op jit(solution)/shard_map/jit(cholesky)/cholesky | solution.py:12
  129.3 0.1 compare_reduce_fusion
  129.4 0.1 select_bitcast_fusion
  129.5 4.9 %custom-call.9 = f32[2,1,32,32]{2,3,1,0:T(8,128)S(1)} custom-call(f32[2,1,32,32]{3,2,1,0:T(8,128)S(1)} %select_bitcast_fusion), custom_call_target="InvertDiagBlocksLowerTriangular" | custom-call | tf_op jit(solution)/shard_map/vmap(jit(_solve_triangular))/triangular_solve | solution.py:13
  134.4 0.3 fusion.5
  134.6 0.2 fusion.13
  134.8 0.0 copy-start.1
  134.8 111.8 %all-reduce.2.cloned.1.call-done = f32[5120,2,32]{0,2,1:T(8,128)} async-done(((f32[5120,2,32]{0,2,1:T(8,128)}), f32[5120,2,32]{0,2,1:T(8,128)}) %all-reduce.2.cloned.1.call-update) | async-done | bytes 1310736 | tf_op jit(solution)/shard_map/psum | solution.py:31
  246.6 2.5 convolution_multiply_fusion
  249.2 0.7 dynamic-slice_bitcast_fusion
  249.9 8.8 %fusion.1 = bf16[1,2,384,5120]{3,2,1,0:T(8,128)(2,1)} fusion(f32[2,32,5120]{2,1,0:T(8,128)S(1)} %convolution_multiply_fusion, f32[2,384,32]{1,2,0:T(8,128)S(1)} %fusion.13, bf16[1,2,384,5120]{3,2,1,0:T(8,128)(2,1)} %param.4, bf16[1,2,384,5120]{3,2,1,0:T(8,128)(2,1)} %param.3), kind=kOutput, calls=%fused_computation.3 | convolution fusion | flops 279535616 | bytes 25001984 | tf_op jit(solution)/shard_map/mrk,dmk->mrd/dot_general | solution.py:39
  258.7 0.0 copy-done.1
  (5 shorter events, 0.1 us)
Async XLA Ops:
  7.2 1.1 copy-start
  7.2 239.4 %all-reduce.2.cloned.1.call-start = ((), (), s32[]{:S(2)}) async-start(), calls=%async_computation | async-start | bytes 2621440 | tf_op jit(solution)/shard_map/psum | solution.py:31
  134.8 123.8 %copy-start.1 = (f32[2,384,32]{1,2,0:T(8,128)}, f32[2,384,32]{1,2,0:T(8,128)S(1)}, u32[]{:S(2)}) copy-start(f32[2,384,32]{1,2,0:T(8,128)S(1)} %fusion.13) | copy-start | bytes 294916
Sparse Core Ops, SparseCore 0:
  87.9 158.6 all-reduce.1
where the time goes:
time: 266 us
  waiting for transfers between devices  112 us (42%)
  blocking collectives  97.8 us (37%)
  matrix products  28.6 us (11%)
  between operations  14.1 us (5%)
  other arithmetic  11.3 us (4%)
    psum x1, waiting for transfers between devices, compress(): total_sum = lax.psum(projected, ('dp', 'tensor'))  112 us
    psum x1, blocking collectives, compress(): summed = lax.psum(partial_p.astype(jnp.bfloat16), 'dp').astype(jnp.float32)  62.7 us
    psum x1, blocking collectives, compress(): gram_full = lax.psum(gram_part, 'tensor')  35.1 us
    dot_general x1, matrix products, compress(): jnp.einsum('mrd,mrk->dmk', corrected, p_round, preferred_element_type=jnp...  8.83 us
    dot_general x1, matrix products, compress(): jnp.einsum('mrk,dmk->mrd', p_factor_round, q_round, preferred_element_typ...  8.79 us
    dot_general x1, matrix products, compress(): jnp.einsum('mrd,dmk->mrk', corrected, q_start, preferred_element_type=jnp...  7.9 us
    another operation x4, other arithmetic, inverse_factor(): factor = jnp.linalg.cholesky(shifted)  6.01 us
  transfers between devices with their start and end apart: 1, of which 1 were waited for; matrix products, arithmetic and copies ran while one was open for 4% of the time, Pallas kernels for 0%

commit v1 on v0

v1 whole, which is shorter than its diff:
```python
import jax
import jax.numpy as jnp
from jax import lax
from jax.experimental import pallas as pl
from jax.experimental.pallas import tpu as pltpu
from jax.sharding import PartitionSpec as P

F32 = jnp.float32
BF16 = jnp.bfloat16
HIGHEST = lax.Precision.HIGHEST
NN = (((1,), (0,)), ((), ()))
NT = (((1,), (1,)), ((), ()))
VMEM_BYTES = 32 * 1024 * 1024

MATS, ROWS, WIDTH, RANK = 2, 384, 5120, 32
BOTH = MATS * RANK
HALF = WIDTH // 2
LANES = 2 * BOTH
DP, TENSOR = 16, 8
DEVICES = DP * TENSOR
HEAD = 16 * DEVICES
CHUNK = 24
FIRST_STEP = 512
LAST_STEP = 512


def left_kernel(grad_ref, error_ref, q_ref, corrected_ref, out_ref, acc_ref):
    step = pl.program_id(0)

    @pl.when(step == 0)
    def _():
        acc_ref[...] = jnp.zeros_like(acc_ref)

    columns = pl.ds(pl.multiple_of(step * FIRST_STEP, FIRST_STEP), FIRST_STEP)
    for m in range(MATS):
        corrected = (grad_ref[m].astype(F32) + error_ref[m].astype(F32)).astype(BF16)
        corrected_ref[m, :, columns] = corrected
        acc_ref[m] += lax.dot_general(corrected, q_ref[m], NT, preferred_element_type=F32)

    @pl.when(step == pl.num_programs(0) - 1)
    def _():
        part = jnp.concatenate([acc_ref[m].T for m in range(MATS)], axis=0).astype(BF16)
        for r in range(DP):
            out_ref[r] = part


def right_kernel(parts_ref, corrected_ref, out_ref, summed_ref, turned_ref, tail_ref, gram_ref):
    summed = parts_ref[0].astype(F32)
    for r in range(1, DP):
        summed = summed + parts_ref[r].astype(F32)
    summed_ref[...] = summed
    left = [summed[m * RANK : (m + 1) * RANK] for m in range(MATS)]
    left_round = [x.astype(BF16) for x in left]

    gram = jnp.concatenate(
        [lax.dot_general(x, x, NT, precision=HIGHEST, preferred_element_type=F32) for x in left], axis=0
    )
    gram_ref[...] = jnp.concatenate([gram[16 * a : 16 * a + 16] for a in range(4)], axis=1)
    row = gram_ref[pl.ds(lax.axis_index("dp"), 1), :]
    high = row.astype(BF16).astype(F32)
    middle = (row - high).astype(BF16).astype(F32)
    low = row - high - middle
    terms = jnp.concatenate([high, middle, low, jnp.zeros_like(row)], axis=0)

    def columns_step(i, carry):
        products = []
        for h in range(2):
            columns = pl.ds(pl.multiple_of(HALF * h + 256 * i, 256), 256)
            for m in range(MATS):
                products.append(
                    lax.dot_general(left_round[m], corrected_ref[m, :, columns], NN, preferred_element_type=F32)
                )
        turned_ref[pl.ds(pl.multiple_of(256 * i, 256), 256), :] = jnp.concatenate(products, axis=0).T
        return carry

    lax.fori_loop(0, HALF // 256, columns_step, 0, unroll=2)

    for c in range(DEVICES):
        tail_ref[c, 0:4, :] = turned_ref[HEAD + 4 * c : HEAD + 4 * c + 4, :]
    tail_ref[:, 4:8, :] = jnp.broadcast_to(terms[None], (DEVICES, 4, LANES))
    for g in range(DEVICES // 16):
        head = turned_ref[256 * g : 256 * g + 256, :].reshape(16, 16, LANES)
        out_ref[16 * g : 16 * g + 16] = jnp.concatenate(
            [head, tail_ref[16 * g : 16 * g + 16]], axis=1
        ).astype(BF16)


def inverse_factors(grams):
    row = lax.broadcasted_iota(jnp.int32, (RANK, LANES), 0)
    lane = lax.broadcasted_iota(jnp.int32, (RANK, LANES), 1)
    first = (lane // RANK) % 2 == 0
    eye = (lane % RANK == row).astype(F32)
    square = jnp.concatenate(list(grams) + [jnp.zeros((RANK, LANES - BOTH), F32)], axis=1)
    diagonal = square * eye
    trace = [
        jnp.sum(jnp.where(lane // RANK == m, diagonal, 0.0), axis=(0, 1), keepdims=True) for m in range(MATS)
    ]
    shift = 1e-05 * jnp.where(first, trace[0], trace[1]) / RANK
    work = square + jnp.where(lane < BOTH, shift * eye, eye)
    for j in range(RANK - 1):
        column = jnp.where(first, work[:, j : j + 1], work[:, RANK + j : RANK + j + 1])
        pivot_row = work[j : j + 1, :]
        scaled = pivot_row / column[j : j + 1, :]
        work = work - jnp.where(row > j, column, 0.0) * scaled
    pivots = work * eye
    pivot = [
        jnp.sum(jnp.where(lane // RANK == m, pivots, 0.0), axis=1, keepdims=True) for m in range(MATS)
    ]
    return work / jnp.sqrt(jnp.where(first, pivot[0], pivot[1]))


def factor_kernel(parts_ref, summed_ref, out_ref, p_ref, gram_ref):
    total = jnp.zeros((CHUNK, LANES), F32)
    for r in range(DP):
        block = parts_ref[TENSOR * r].astype(F32)
        for t in range(1, TENSOR):
            block = block + parts_ref[TENSOR * r + t].astype(F32)
        total = total + block
        gram_ref[r : r + 1, :] = block[20:21] + block[21:22] + block[22:23]
    gram = gram_ref[...]
    gram = jnp.concatenate([gram[:, RANK * a : RANK * a + RANK] for a in range(4)], axis=0)
    inverse = inverse_factors([gram[m * RANK : (m + 1) * RANK] for m in range(MATS)])

    lane = lax.broadcasted_iota(jnp.int32, (RANK, LANES), 1)
    turned = pltpu.roll(inverse, BOTH, 1)
    weights = jnp.concatenate(
        [
            jnp.where(lane // RANK == 2 * h + m, inverse if h else turned, 0.0)
            for h in range(2)
            for m in range(MATS)
        ],
        axis=0,
    )
    right = lax.dot_general(total, weights, NT, precision=HIGHEST, preferred_element_type=F32) / DP
    row = lax.broadcasted_iota(jnp.int32, (CHUNK, LANES), 0)
    right = jnp.where(row < 20, right, 0.0).astype(BF16)
    out_ref[...] = jnp.broadcast_to(right[None], (DEVICES, CHUNK, LANES))
    p_ref[...] = lax.dot_general(
        weights[:BOTH, :BOTH], summed_ref[...], NN, precision=HIGHEST, preferred_element_type=F32
    )


def error_kernel(right_ref, p_ref, corrected_ref, out_ref, q_ref, wide_ref, turned_ref, left_ref):
    step = pl.program_id(0)

    @pl.when(step == 0)
    def _():
        for g in range(DEVICES // 16):
            block = right_ref[16 * g : 16 * g + 16].astype(F32)
            wide_ref[256 * g : 256 * g + 256, :] = block[:, 0:16].reshape(256, LANES)
            for c in range(16):
                start = HEAD + 4 * (16 * g + c)
                wide_ref[start : start + 4, :] = block[c, 16:20]
        wide_ref[HALF:, :] = jnp.zeros((LANES, LANES), F32)
        turned_ref[...] = wide_ref[:HALF, :].astype(BF16)
        p = p_ref[...].T
        p = jnp.concatenate([p, p], axis=1)
        lane = lax.broadcasted_iota(jnp.int32, (ROWS, LANES), 1)
        for h in range(2):
            for m in range(MATS):
                left_ref[h, ROWS * m : ROWS * m + ROWS, :] = jnp.where(
                    lane // RANK == 2 * h + m, p, 0.0
                ).astype(BF16)
        me = lax.axis_index(("dp", "tensor"))
        share = WIDTH // DEVICES
        start = pl.multiple_of(share * (me % (DEVICES // 2)), 8)
        own = wide_ref[pl.ds(start, LANES), :].T
        q_ref[...] = jnp.where(me < DEVICES // 2, own[:BOTH, :share], own[BOTH:, :share])

    per_half = HALF // LAST_STEP
    h = step // per_half
    rows = pl.ds(pl.multiple_of((step % per_half) * LAST_STEP, LAST_STEP), LAST_STEP)
    columns = pl.ds(pl.multiple_of(step * LAST_STEP, LAST_STEP), LAST_STEP)
    rebuilt = lax.dot_general(left_ref[h], turned_ref[rows, :], NT, preferred_element_type=F32)
    for m in range(MATS):
        out_ref[m] = (
            corrected_ref[m, :, columns].astype(F32) - rebuilt[ROWS * m : ROWS * m + ROWS]
        ).astype(BF16)


def params(grid=True):
    return pltpu.CompilerParams(
        dimension_semantics=("arbitrary",) if grid else None, vmem_limit_bytes=VMEM_BYTES
    )


WHOLE = pl.BlockSpec(memory_space=pltpu.VMEM)


def local(grad, error, q_init):
    q_turned = q_init.transpose(1, 2, 0)
    step_spec = pl.BlockSpec((MATS, ROWS, FIRST_STEP), lambda i: (0, 0, i))
    corrected, part = pl.pallas_call(
        left_kernel,
        grid=(WIDTH // FIRST_STEP,),
        in_specs=[step_spec, step_spec, pl.BlockSpec((MATS, RANK, FIRST_STEP), lambda i: (0, 0, i))],
        out_specs=[WHOLE, WHOLE],
        out_shape=[
            pltpu.VMEM((MATS, ROWS, WIDTH), BF16),
            jax.ShapeDtypeStruct((DP, BOTH, ROWS), BF16),
        ],
        scratch_shapes=[pltpu.VMEM((MATS, ROWS, RANK), F32)],
        compiler_params=params(),
        name="left_product",
    )(grad[0], error[0], q_turned)

    parts = lax.all_to_all(part, "dp", 0, 0, tiled=True)

    partial_q, summed = pl.pallas_call(
        right_kernel,
        in_specs=[WHOLE, WHOLE],
        out_specs=[WHOLE, WHOLE],
        out_shape=[
            jax.ShapeDtypeStruct((DEVICES, CHUNK, LANES), BF16),
            jax.ShapeDtypeStruct((BOTH, ROWS), F32),
        ],
        scratch_shapes=[
            pltpu.VMEM((HALF, LANES), F32),
            pltpu.VMEM((DEVICES, 8, LANES), F32),
            pltpu.VMEM((16, LANES), F32),
        ],
        compiler_params=params(False),
        name="right_product",
    )(parts, corrected)

    partial_q = lax.all_to_all(partial_q, ("dp", "tensor"), 0, 0, tiled=True)

    q_own, p_turned = pl.pallas_call(
        factor_kernel,
        in_specs=[WHOLE, WHOLE],
        out_specs=[WHOLE, WHOLE],
        out_shape=[
            jax.ShapeDtypeStruct((DEVICES, CHUNK, LANES), BF16),
            jax.ShapeDtypeStruct((BOTH, ROWS), F32),
        ],
        scratch_shapes=[pltpu.VMEM((16, LANES), F32)],
        compiler_params=params(False),
        name="factor",
    )(partial_q, summed)

    q_all = lax.all_to_all(q_own, ("dp", "tensor"), 0, 0, tiled=True)

    new_error, q_factor = pl.pallas_call(
        error_kernel,
        grid=(WIDTH // LAST_STEP,),
        in_specs=[WHOLE, WHOLE, WHOLE],
        out_specs=[pl.BlockSpec((MATS, ROWS, LAST_STEP), lambda i: (0, 0, i)), WHOLE],
        out_shape=[
            jax.ShapeDtypeStruct((MATS, ROWS, WIDTH), BF16),
            jax.ShapeDtypeStruct((BOTH, WIDTH // DEVICES), F32),
        ],
        scratch_shapes=[
            pltpu.VMEM((HALF + LANES, LANES), F32),
            pltpu.VMEM((HALF, LANES), BF16),
            pltpu.VMEM((2, MATS * ROWS, LANES), BF16),
        ],
        compiler_params=params(),
        name="new_error",
    )(q_all, p_turned, corrected)

    return (
        new_error[None],
        p_turned.reshape(MATS, RANK, ROWS).transpose(0, 2, 1),
        q_factor.reshape(MATS, RANK, WIDTH // DEVICES).transpose(2, 0, 1),
    )


def solution(mesh):
    in_specs = (P("dp", None, "tensor", None), P("dp", None, "tensor", None), P())
    out_specs = (
        P("dp", None, "tensor", None),
        P(None, "tensor", None),
        P(("dp", "tensor"), None, None),
    )
    return jax.shard_map(local, mesh=mesh, in_specs=in_specs, out_specs=out_specs, check_vma=False)
```

time: 266 us -> 95 us (0.36)
  waiting for transfers between devices: 112 us -> 0 us
  blocking collectives: 97.8 us -> 66.2 us
  matrix products: 28.6 us -> 0 us
  Pallas kernels: 0 us -> 22.5 us
  between operations: 14.1 us -> 0.66 us
  other arithmetic: 11.3 us -> 0 us
  local copies, waits for them, and re-layouts: 1.82 us -> 5.21 us
    psum x1 -> x0, waiting for transfers between devices: 112 us -> none  [compress(): total_sum = lax.psum(projected, ('dp', 'tensor'))]
    psum x2 -> x0, blocking collectives: 97.8 us -> none  [the longest x1 62.7 us: compress(): summed = lax.psum(partial_p.astype(jnp.bfloat16), 'dp').astype(jnp.float32)]
    all_to_all x0 -> x3, blocking collectives: none -> 66.2 us  [the longest x1 23.7 us: local(): partial_q = lax.all_to_all(partial_q, ('dp', 'tensor'), 0, 0, tiled=True)]
    dot_general x6 -> x0, matrix products: 28.4 us -> none  [the longest x1 8.83 us: compress(): jnp.einsum('mrd,mrk->dmk', corrected, p_round, preferred_element_type=jnp...]
    pallas_call x0 -> x4, Pallas kernels: none -> 22.5 us  [the longest x1 8.69 us: local(): pl.pallas_call(left_kernel, grid=(WIDTH // FIRST_STEP,), in_specs=[step_s...]
    another operation x7 -> x0, other arithmetic: 11 us -> none  [the longest x4 6.01 us: inverse_factor(): factor = jnp.linalg.cholesky(shifted)]
    unnamed x4 -> x6, local copies, waits for them, and re-layouts: 1.05 us -> 5.21 us
  transfers between devices with their start and end apart: 1 -> 0, of which waited for: 1 -> 0; matrix products, arithmetic and copies ran while one was open for 4% -> 0% of each run, Pallas kernels for 0% -> 0%
where the time goes in v1:
time: 95 us; the launch traced here: 94.5 us
  blocking collectives  66.2 us (70%)
  Pallas kernels  22.5 us (24%)
  local copies, waits for them, and re-layouts  5.21 us (5%)
    all_to_all x1, blocking collectives, local(): partial_q = lax.all_to_all(partial_q, ('dp', 'tensor'), 0, 0, tiled=True)  23.7 us
    all_to_all x1, blocking collectives, local(): parts = lax.all_to_all(part, 'dp', 0, 0, tiled=True)  21.8 us
    all_to_all x1, blocking collectives, local(): q_all = lax.all_to_all(q_own, ('dp', 'tensor'), 0, 0, tiled=True)  20.8 us
    pallas_call x1, Pallas kernels, local(): pl.pallas_call(left_kernel, grid=(WIDTH // FIRST_STEP,), in_specs=[step_s...  8.69 us
    pallas_call x1, Pallas kernels, local(): pl.pallas_call(error_kernel, grid=(WIDTH // LAST_STEP,), in_specs=[WHOLE,...  6.9 us
    unnamed x6, local copies, waits for them, and re-layouts  5.21 us
    pallas_call x1, Pallas kernels, local(): pl.pallas_call(factor_kernel, in_specs=[WHOLE, WHOLE], out_specs=[WHOLE,...  4.06 us
    pallas_call x1, Pallas kernels, local(): pl.pallas_call(right_kernel, in_specs=[WHOLE, WHOLE], out_specs=[WHOLE, W...  2.8 us

profile of v1, /device:TPU:1, one launch (start us, length us, event | category | flops | bytes accessed | tf_op | source)
XLA Modules:
  0.0 94.5 jit_solution(17042508487338998386)
XLA Ops:
  0.6 0.0 copy-start
  0.6 3.2 %copy-done = bf16[1,2,384,5120]{3,2,1,0:T(8,128)(2,1)S(1)} copy-done((bf16[1,2,384,5120]{3,2,1,0:T(8,128)(2,1)S(1)}, bf16[1,2,384,5120]{3,2,1,0:T(8,128)(2,1)}, u32[]{:S(2)}) %copy-start) | copy-done | bytes 7864344
  3.9 0.0 copy-start.1
  3.9 1.1 %copy-done.1 = bf16[5120,2,32]{0,2,1:T(8,128)(2,1)S(1)} copy-done((bf16[5120,2,32]{0,2,1:T(8,128)(2,1)S(1)}, bf16[5120,2,32]{0,2,1:T(8,128)(2,1)}, u32[]{:S(2)}) %copy-start.1) | copy-done | bytes 655384
  5.0 8.7 %left_product.1 = (bf16[2,384,5120]{2,1,0:T(8,128)(2,1)S(1)}, bf16[16,64,384]{2,1,0:T(8,128)(2,1)S(1)}) custom-call(bf16[2,384,5120]{2,1,0:T(8,128)(2,1)S(1)} %bitcast.10, bf16[2,384,5120]{2,1,0:T(8,128)(2,1)} %bitcast.13, bf16[2,32,5120]{2,1,0:T(8,128)(2,1)S(1)} %bitcast.11), custom_call_target="tpu_custom_call" | custom-call | tf_op jit(solution)/shard_map/left_product/pallas_call | solution.py:193
  13.7 21.8 %all_to_all.15.parts_ref = bf16[16,64,384]{2,1,0:T(8,128)(2,1)S(1)} all-to-all(bf16[16,64,384]{2,1,0:T(8,128)(2,1)S(1)} %get-tuple-element.11), channel_id=1, replica_groups=mesh['dp'=16,'tensor'=8] {'dp'}, dimensions={0} | all-to-all | bytes 1572864 | tf_op jit(solution)/shard_map/all_to_all | solution.py:207
  35.4 2.8 %right_product.1 = (bf16[128,24,128]{2,1,0:T(8,128)(2,1)S(1)}, f32[64,384]{1,0:T(8,128)S(1)}) custom-call(bf16[16,64,384]{2,1,0:T(8,128)(2,1)S(1)} %all_to_all.15.parts_ref, bf16[2,384,5120]{2,1,0:T(8,128)(2,1)S(1)} %get-tuple-element.12.corrected_ref), custom_call_target="tpu_custom_call" | custom-call | tf_op jit(solution)/shard_map/right_product/pallas_call | solution.py:209
  38.2 23.7 %all_to_all.16.parts_ref = bf16[128,24,128]{2,1,0:T(8,128)(2,1)S(1)} all-to-all(bf16[128,24,128]{2,1,0:T(8,128)(2,1)S(1)} %get-tuple-element.13), channel_id=1, replica_groups=mesh['dp'=16,'tensor'=8] {'dp','tensor'}, dimensions={0} | all-to-all | bytes 1572864 | tf_op jit(solution)/shard_map/all_to_all | solution.py:226
  61.9 4.1 %factor.1 = (bf16[128,24,128]{2,1,0:T(8,128)(2,1)S(1)}, f32[64,384]{1,0:T(8,128)}) custom-call(bf16[128,24,128]{2,1,0:T(8,128)(2,1)S(1)} %all_to_all.16.parts_ref, f32[64,384]{1,0:T(8,128)S(1)} %get-tuple-element.14.summed_ref), custom_call_target="tpu_custom_call" | custom-call | tf_op jit(solution)/shard_map/factor/pallas_call | solution.py:228
  66.0 20.8 %all_to_all.17.right_ref = bf16[128,24,128]{2,1,0:T(8,128)(2,1)S(1)} all-to-all(bf16[128,24,128]{2,1,0:T(8,128)(2,1)S(1)} %get-tuple-element.15), channel_id=1, replica_groups=mesh['dp'=16,'tensor'=8] {'dp','tensor'}, dimensions={0} | all-to-all | bytes 1572864 | tf_op jit(solution)/shard_map/all_to_all | solution.py:241
  86.7 0.0 copy-start.2
  86.7 0.9 copy-done.2
  87.6 6.9 %new_error.1 = (bf16[2,384,5120]{2,1,0:T(8,128)(2,1)}, f32[64,40]{1,0:T(8,128)}) custom-call(bf16[128,24,128]{2,1,0:T(8,128)(2,1)S(1)} %all_to_all.17.right_ref, f32[64,384]{1,0:T(8,128)S(1)} %copy-done.2, bf16[2,384,5120]{2,1,0:T(8,128)(2,1)S(1)} %get-tuple-element.12.corrected_ref), custom_call_target="tpu_custom_call" | custom-call | tf_op jit(solution)/shard_map/new_error/pallas_call | solution.py:243
Async XLA Ops:
  0.6 3.2 %copy-start = (bf16[1,2,384,5120]{3,2,1,0:T(8,128)(2,1)S(1)}, bf16[1,2,384,5120]{3,2,1,0:T(8,128)(2,1)}, u32[]{:S(2)}) copy-start(bf16[1,2,384,5120]{3,2,1,0:T(8,128)(2,1)} %param.3) | copy-start | bytes 23592964
  3.9 1.1 %copy-start.1 = (bf16[5120,2,32]{0,2,1:T(8,128)(2,1)S(1)}, bf16[5120,2,32]{0,2,1:T(8,128)(2,1)}, u32[]{:S(2)}) copy-start(bf16[5120,2,32]{0,2,1:T(8,128)(2,1)} %param.5) | copy-start | bytes 1966084
  86.7 0.9 copy-start.2

commit v2 on v0

v2 whole, which is shorter than its diff:
```python
import jax
import jax.numpy as jnp
from jax import lax
from jax.experimental import pallas as pl
from jax.experimental.pallas import tpu as pltpu
from jax.sharding import PartitionSpec as P

F32 = jnp.float32
BF16 = jnp.bfloat16
HIGHEST = lax.Precision.HIGHEST
NN = (((1,), (0,)), ((), ()))
NT = (((1,), (1,)), ((), ()))
VMEM_BYTES = 36 * 1024 * 1024

MATS, ROWS, WIDTH, RANK = 2, 384, 5120, 32
BOTH = MATS * RANK
HALF, QUARTER = WIDTH // 2, WIDTH // 4
LANES = 2 * BOTH
DP, TENSOR = 16, 8
DEVICES = DP * TENSOR
CHIPS = DEVICES // 2
CHIPS_X = TENSOR // 2
SHARE = WIDTH // DEVICES
HEAD = 16 * CHIPS
CHUNK = 24
STEP = 512
TILE = 256
BOTH_AXES = ("dp", "tensor")
CORE_PAIRS = [(i, i ^ 1) for i in range(TENSOR)]
SAME_CORE = [[i for i in range(DEVICES) if i % 2 == core] for core in range(2)]


def columns_at(start, size):
    return pl.ds(pl.multiple_of(start, TILE), size)


def left_kernel(grad_ref, error_ref, q_ref, corrected_ref, out_ref, error_vmem, q_vmem, acc_ref, sems):
    starts = range(0, WIDTH, STEP)
    copies = []
    for i, start in enumerate(starts):
        columns = pl.ds(start, STEP)
        pairs = [(q_ref, q_vmem), (grad_ref, corrected_ref), (error_ref, error_vmem)]
        copies.append(
            [
                pltpu.make_async_copy(source.at[:, :, columns], target.at[:, :, columns], sems.at[n, i])
                for n, (source, target) in enumerate(pairs)
            ]
        )
        for copy in copies[-1]:
            copy.start()
    for i, start in enumerate(starts):
        columns = pl.ds(start, STEP)
        for copy in copies[i]:
            copy.wait()
        for m in range(MATS):
            corrected = (corrected_ref[m, :, columns].astype(F32) + error_vmem[m, :, columns].astype(F32)).astype(BF16)
            corrected_ref[m, :, columns] = corrected
            product = lax.dot_general(corrected, q_vmem[m, :, columns], NT, preferred_element_type=F32)
            if i == 0:
                acc_ref[m] = product
            else:
                acc_ref[m] += product
    part = jnp.concatenate([acc_ref[m].T for m in range(MATS)], axis=0).astype(BF16)
    for r in range(DP):
        out_ref[r] = part


def split_row(row):
    high = row.astype(BF16).astype(F32)
    middle = (row - high).astype(BF16).astype(F32)
    low = row - high - middle
    return jnp.concatenate([high, middle, low, jnp.zeros_like(row)], axis=0)


def half_product(left, corrected_ref, core, turned_ref):
    def columns_step(i, carry):
        products = []
        for g in range(2):
            columns = columns_at(HALF * core + QUARTER * g + TILE * i, TILE)
            for m in range(MATS):
                products.append(
                    lax.dot_general(left[m], corrected_ref[m, :, columns], NN, preferred_element_type=F32)
                )
        turned_ref[columns_at(TILE * i, TILE), :] = jnp.concatenate(products, axis=0).T
        return carry

    lax.fori_loop(0, QUARTER // TILE, columns_step, 0, unroll=True)


def chunked(turned_ref, tail_ref, terms):
    for c in range(CHIPS):
        tail_ref[c, 0:4, :] = turned_ref[HEAD + 4 * c : HEAD + 4 * c + 4, :]
    tail_ref[:, 4:8, :] = jnp.broadcast_to(terms[None], (CHIPS, 4, LANES))
    for n in range(CHIPS // 16):
        head = turned_ref[256 * n : 256 * n + 256, :].reshape(16, 16, LANES)
        yield 16 * n, jnp.concatenate([head, tail_ref[16 * n : 16 * n + 16]], axis=1)


def other_half_kernel(
    parts_ref, corrected_ref, out_ref, summed_ref, row_ref, turned_ref, tail_ref, gram_ref
):
    summed = parts_ref[0].astype(F32)
    for r in range(1, DP):
        summed = summed + parts_ref[r].astype(F32)
    summed_ref[...] = summed
    left = [summed[m * RANK : (m + 1) * RANK] for m in range(MATS)]
    core = lax.axis_index("tensor") % 2
    half_product([x.astype(BF16) for x in left], corrected_ref, 1 - core, turned_ref)

    gram = jnp.concatenate(
        [lax.dot_general(x, x, NT, precision=HIGHEST, preferred_element_type=F32) for x in left], axis=0
    )
    gram_ref[...] = jnp.concatenate([gram[16 * a : 16 * a + 16] for a in range(4)], axis=1)
    row = gram_ref[pl.ds(lax.axis_index("dp"), 1), :]
    row_ref[...] = jnp.broadcast_to(row, row_ref.shape)
    for start, chunks in chunked(turned_ref, tail_ref, split_row(row)):
        out_ref[start : start + 16] = chunks.astype(BF16)


def own_half_kernel(summed_ref, corrected_ref, out_ref, turned_ref, tail_ref):
    left = [summed_ref[m * RANK : (m + 1) * RANK].astype(BF16) for m in range(MATS)]
    half_product(left, corrected_ref, lax.axis_index("tensor") % 2, turned_ref)
    for start, chunks in chunked(turned_ref, tail_ref, jnp.zeros((4, LANES), F32)):
        out_ref[start : start + 16] = chunks


def pair_sum_kernel(own_ref, other_ref, row_ref, out_ref):
    other = other_ref[0].astype(F32)
    row = row_ref[0:1] + (other[20:21] + other[21:22] + other[22:23])
    terms = jnp.concatenate([jnp.zeros((20, LANES), F32), split_row(row)], axis=0)
    is_right = lax.broadcasted_iota(jnp.int32, (1, CHUNK, LANES), 1) < 20
    for start in range(0, CHIPS, 8):
        both = own_ref[start : start + 8] + other_ref[start : start + 8].astype(F32)
        out_ref[start : start + 8] = jnp.where(is_right, both, terms[None]).astype(BF16)


def inverse_factors(grams):
    row = lax.broadcasted_iota(jnp.int32, (RANK, LANES), 0)
    lane = lax.broadcasted_iota(jnp.int32, (RANK, LANES), 1)
    first = (lane // RANK) % 2 == 0
    eye = (lane % RANK == row).astype(F32)
    square = jnp.concatenate(list(grams) + [jnp.zeros((RANK, LANES - BOTH), F32)], axis=1)
    diagonal = square * eye
    trace = [
        jnp.sum(jnp.where(lane // RANK == m, diagonal, 0.0), axis=(0, 1), keepdims=True) for m in range(MATS)
    ]
    shift = 1e-05 * jnp.where(first, trace[0], trace[1]) / RANK
    work = square + jnp.where(lane < BOTH, shift * eye, eye)
    for j in range(RANK - 1):
        column = jnp.where(first, work[:, j : j + 1], work[:, RANK + j : RANK + j + 1])
        pivot_row = work[j : j + 1, :]
        scaled = pivot_row / column[j : j + 1, :]
        work = work - jnp.where(row > j, column, 0.0) * scaled
    pivots = work * eye
    pivot = [
        jnp.sum(jnp.where(lane // RANK == m, pivots, 0.0), axis=1, keepdims=True) for m in range(MATS)
    ]
    return work / jnp.sqrt(jnp.where(first, pivot[0], pivot[1]))


def factor_kernel(parts_ref, summed_ref, out_ref, p_ref, left_ref, gram_ref):
    total = jnp.zeros((CHUNK, LANES), F32)
    for r in range(DP):
        block = parts_ref[CHIPS_X * r].astype(F32)
        for x in range(1, CHIPS_X):
            block = block + parts_ref[CHIPS_X * r + x].astype(F32)
        total = total + block
        gram_ref[r : r + 1, :] = block[20:21] + block[21:22] + block[22:23]
    gram = gram_ref[...]
    gram = jnp.concatenate([gram[:, RANK * a : RANK * a + RANK] for a in range(4)], axis=0)
    inverse = inverse_factors([gram[m * RANK : (m + 1) * RANK] for m in range(MATS)])

    lane = lax.broadcasted_iota(jnp.int32, (RANK, LANES), 1)
    turned = pltpu.roll(inverse, BOTH, 1)
    weights = jnp.concatenate(
        [
            jnp.where(lane // RANK == 2 * g + m, inverse if g else turned, 0.0)
            for g in range(2)
            for m in range(MATS)
        ],
        axis=0,
    )
    right = lax.dot_general(total, weights, NT, precision=HIGHEST, preferred_element_type=F32) / DP
    row = lax.broadcasted_iota(jnp.int32, (CHUNK, LANES), 0)
    right = jnp.where(row < 20, right, 0.0).astype(BF16)
    out_ref[...] = jnp.broadcast_to(right[None], out_ref.shape)
    p = lax.dot_general(
        weights[:BOTH, :BOTH], summed_ref[...], NN, precision=HIGHEST, preferred_element_type=F32
    )
    p_ref[...] = p
    p = p.T
    p = jnp.concatenate([p, p], axis=1)
    lane = lax.broadcasted_iota(jnp.int32, (ROWS, LANES), 1)
    for g in range(2):
        for m in range(MATS):
            left_ref[g, ROWS * m : ROWS * m + ROWS, :] = jnp.where(lane // RANK == 2 * g + m, p, 0.0).astype(BF16)


def half_error(right_ref, left_ref, corrected_ref, out_ref, core, wide_ref, turned_ref, stage_ref, sems):
    for n in range(CHIPS // 16):
        block = right_ref[16 * n : 16 * n + 16].astype(F32)
        wide_ref[256 * n : 256 * n + 256, :] = block[:, 0:16].reshape(256, LANES)
        for c in range(16):
            start = HEAD + 4 * (16 * n + c)
            wide_ref[start : start + 4, :] = block[c, 16:20]
    turned_ref[...] = wide_ref[:QUARTER, :].astype(BF16)

    copies = []
    for i in range(QUARTER // TILE):
        for g in range(2):
            columns = columns_at(HALF * core + QUARTER * g + TILE * i, TILE)
            local_columns = pl.ds(QUARTER * g + TILE * i, TILE)
            rebuilt = lax.dot_general(
                left_ref[g], turned_ref[TILE * i : TILE * i + TILE, :], NT, preferred_element_type=F32
            )
            for m in range(MATS):
                stage_ref[m, :, local_columns] = (
                    corrected_ref[m, :, columns].astype(F32) - rebuilt[ROWS * m : ROWS * m + ROWS]
                ).astype(BF16)
            copy = pltpu.make_async_copy(
                stage_ref.at[:, :, local_columns], out_ref.at[:, :, columns], sems.at[i, g]
            )
            copy.start()
            copies.append(copy)

    me = lax.axis_index("dp") * TENSOR + lax.axis_index("tensor")
    wide_ref[QUARTER:, :] = jnp.zeros((LANES, LANES), F32)
    start = pl.multiple_of(SHARE * (me % (DEVICES // 4)), 8)
    own = wide_ref[pl.ds(start, LANES), :].T
    upper = (me // (DEVICES // 4)) % 2 == 1
    own = jnp.where(upper, own[BOTH:, :SHARE], own[:BOTH, :SHARE])
    for copy in copies:
        copy.wait()
    return own, me // CHIPS == core


def own_error_kernel(right_ref, left_ref, corrected_ref, out_ref, q_ref, *scratch):
    core = lax.axis_index("tensor") % 2
    own, _ = half_error(right_ref, left_ref, corrected_ref, out_ref, core, *scratch)
    q_ref[...] = own


def other_error_kernel(right_ref, left_ref, corrected_ref, q_own_ref, error_ref, out_ref, q_ref, *scratch):
    del error_ref
    core = 1 - lax.axis_index("tensor") % 2
    own, here = half_error(right_ref, left_ref, corrected_ref, out_ref, core, *scratch)
    q_ref[...] = jnp.where(here, own, q_own_ref[...])


WHOLE = pl.BlockSpec(memory_space=pltpu.VMEM)
IN_HBM = pl.BlockSpec(memory_space=pltpu.HBM)


def call(kernel, name, in_specs, out_shape, out_specs=None, scratch=(), flops=0, **extra):
    return pl.pallas_call(
        kernel,
        in_specs=in_specs,
        out_specs=out_specs or [WHOLE] * len(out_shape),
        out_shape=out_shape,
        scratch_shapes=list(scratch),
        compiler_params=pltpu.CompilerParams(vmem_limit_bytes=VMEM_BYTES),
        cost_estimate=pl.CostEstimate(flops=flops, bytes_accessed=4 << 20, transcendentals=0),
        name=name,
        **extra,
    )


def in_hbm(x):
    return pltpu.with_memory_space_constraint(x, pltpu.HBM)


def local(grad, error, q_init):
    steps = WIDTH // STEP
    corrected, part = call(
        left_kernel,
        "left_product",
        [IN_HBM] * 3,
        [pltpu.VMEM((MATS, ROWS, WIDTH), BF16), pltpu.VMEM((DP, BOTH, ROWS), BF16)],
        scratch=[
            pltpu.VMEM((MATS, ROWS, WIDTH), BF16),
            pltpu.VMEM((MATS, RANK, WIDTH), BF16),
            pltpu.VMEM((MATS, ROWS, RANK), F32),
            pltpu.SemaphoreType.DMA((3, steps)),
        ],
    )(in_hbm(grad[0]), in_hbm(error[0]), in_hbm(q_init.transpose(1, 2, 0)))

    parts = lax.all_to_all(part, "dp", 0, 0, tiled=True)

    turned = pltpu.VMEM((QUARTER, LANES), F32)
    tail = pltpu.VMEM((CHIPS, 8, LANES), F32)
    chunks = pltpu.VMEM((CHIPS, CHUNK, LANES), BF16)
    half_flops = 2 * MATS * ROWS * HALF * RANK
    for_other, summed, gram_row = call(
        other_half_kernel,
        "right_product_other",
        [WHOLE] * 2,
        [chunks, pltpu.VMEM((BOTH, ROWS), F32), pltpu.VMEM((8, LANES), F32)],
        scratch=[turned, tail, pltpu.VMEM((16, LANES), F32)],
        flops=half_flops,
    )(parts, corrected)
    from_other = lax.ppermute(for_other, "tensor", CORE_PAIRS)
    own = call(
        own_half_kernel,
        "right_product_own",
        [WHOLE] * 2,
        [pltpu.VMEM((CHIPS, CHUNK, LANES), F32)],
        scratch=[turned, tail],
        flops=half_flops,
    )(summed, corrected)[0]
    partial_q = call(pair_sum_kernel, "pair_sum", [WHOLE] * 3, [chunks])(own, from_other, gram_row)[0]

    partial_q = lax.all_to_all(partial_q, BOTH_AXES, 0, 0, axis_index_groups=SAME_CORE, tiled=True)

    q_own, p_turned, left = call(
        factor_kernel,
        "factor",
        [WHOLE] * 2,
        [chunks, jax.ShapeDtypeStruct((BOTH, ROWS), F32), pltpu.VMEM((2, MATS * ROWS, LANES), BF16)],
        scratch=[pltpu.VMEM((16, LANES), F32)],
    )(partial_q, summed)

    q_half = lax.all_to_all(q_own, BOTH_AXES, 0, 0, axis_index_groups=SAME_CORE, tiled=True)

    q_other = lax.ppermute(q_half, "tensor", CORE_PAIRS)
    scratch = [
        pltpu.VMEM((QUARTER + LANES, LANES), F32),
        pltpu.VMEM((QUARTER, LANES), BF16),
        pltpu.VMEM((MATS, ROWS, HALF), BF16),
        pltpu.SemaphoreType.DMA((QUARTER // TILE, 2)),
    ]
    error_shape = jax.ShapeDtypeStruct((MATS, ROWS, WIDTH), BF16)
    new_error, q_factor = call(
        own_error_kernel,
        "new_error_own",
        [WHOLE] * 3,
        [error_shape, pltpu.VMEM((BOTH, SHARE), F32)],
        [IN_HBM, WHOLE],
        scratch=scratch,
        flops=half_flops,
    )(q_half, left, corrected)
    new_error, q_factor = call(
        other_error_kernel,
        "new_error_other",
        [WHOLE] * 4 + [IN_HBM],
        [error_shape, jax.ShapeDtypeStruct((BOTH, SHARE), F32)],
        [IN_HBM, WHOLE],
        scratch=scratch,
        flops=half_flops,
        input_output_aliases={4: 0},
    )(q_other, left, corrected, q_factor, new_error)

    return (
        new_error[None],
        p_turned.reshape(MATS, RANK, ROWS).transpose(0, 2, 1),
        q_factor.reshape(MATS, RANK, SHARE).transpose(2, 0, 1),
    )


def solution(mesh):
    in_specs = (P("dp", None, "tensor", None), P("dp", None, "tensor", None), P())
    out_specs = (
        P("dp", None, "tensor", None),
        P(None, "tensor", None),
        P(("dp", "tensor"), None, None),
    )
    return jax.shard_map(local, mesh=mesh, in_specs=in_specs, out_specs=out_specs, check_vma=False)
```

time: 266 us -> 78.5 us (0.30)
  waiting for transfers between devices: 112 us -> 0.44 us
  blocking collectives: 97.8 us -> 54 us
  matrix products: 28.6 us -> 0 us
  Pallas kernels: 0 us -> 18.2 us
  between operations: 14.1 us -> 0.67 us
  other arithmetic: 11.3 us -> 0 us
  starting transfers between devices: 0.04 us -> 5.02 us
    psum x1 -> x0, waiting for transfers between devices: 112 us -> none  [compress(): total_sum = lax.psum(projected, ('dp', 'tensor'))]
    psum x2 -> x0, blocking collectives: 97.8 us -> none  [the longest x1 62.7 us: compress(): summed = lax.psum(partial_p.astype(jnp.bfloat16), 'dp').astype(jnp.float32)]
    all_to_all x0 -> x3, blocking collectives: none -> 54 us  [the longest x1 21.8 us: local(): parts = lax.all_to_all(part, 'dp', 0, 0, tiled=True)]
    dot_general x6 -> x0, matrix products: 28.4 us -> none  [the longest x1 8.83 us: compress(): jnp.einsum('mrd,mrk->dmk', corrected, p_round, preferred_element_type=jnp...]
    pallas_call x0 -> x7, Pallas kernels: none -> 18.2 us  [the longest x1 6.59 us: local(): call(left_kernel, 'left_product', [IN_HBM] * 3, [pltpu.VMEM((MATS, ROWS,...]
    another operation x7 -> x0, other arithmetic: 11 us -> none  [the longest x4 6.01 us: inverse_factor(): factor = jnp.linalg.cholesky(shifted)]
    ppermute x0 -> x2, starting transfers between devices: none -> 5.02 us  [the longest x1 3.22 us: local(): q_other = lax.ppermute(q_half, 'tensor', CORE_PAIRS)]
  transfers between devices with their start and end apart: 1 -> 2, of which waited for: 1 -> 1; matrix products, arithmetic and copies ran while one was open for 4% -> 0% of each run, Pallas kernels for 0% -> 4%
where the time goes in v2:
time: 78.5 us; the launch traced here: 78.3 us
  blocking collectives  54 us (69%)
  Pallas kernels  18.2 us (23%)
  starting transfers between devices  5.02 us (6%)
    all_to_all x1, blocking collectives, local(): parts = lax.all_to_all(part, 'dp', 0, 0, tiled=True)  21.8 us
    all_to_all x1, blocking collectives, local(): lax.all_to_all(partial_q, BOTH_AXES, 0, 0, axis_index_groups=SAME_CORE, t...  17.7 us
    all_to_all x1, blocking collectives, local(): lax.all_to_all(q_own, BOTH_AXES, 0, 0, axis_index_groups=SAME_CORE, tiled...  14.5 us
    pallas_call x1, Pallas kernels, local(): call(left_kernel, 'left_product', [IN_HBM] * 3, [pltpu.VMEM((MATS, ROWS,...  6.59 us
    pallas_call x1, Pallas kernels, local(): call(factor_kernel, 'factor', [WHOLE] * 2, [chunks, jax.ShapeDtypeStruct(...  4.02 us
    ppermute x1, starting transfers between devices, local(): q_other = lax.ppermute(q_half, 'tensor', CORE_PAIRS)  3.22 us
    pallas_call x1, Pallas kernels, local(): call(other_error_kernel, 'new_error_other', [WHOLE] * 4 + [IN_HBM], [erro...  3.04 us
    pallas_call x1, Pallas kernels, local(): call(own_error_kernel, 'new_error_own', [WHOLE] * 3, [error_shape, pltpu....  2.42 us
  transfers between devices with their start and end apart: 2, of which 1 were waited for; matrix products, arithmetic and copies ran while one was open for 0% of the time, Pallas kernels for 4%

profile of v2, /device:TPU:1, one launch (start us, length us, event | category | flops | bytes accessed | tf_op | source)
XLA Modules:
  0.0 78.3 jit_solution(16124265504540523940)
XLA Ops:
  0.6 6.6 %left_product.1 = (bf16[2,384,5120]{2,1,0:T(8,128)(2,1)S(1)}, bf16[16,64,384]{2,1,0:T(8,128)(2,1)S(1)}) custom-call(bf16[2,384,5120]{2,1,0:T(8,128)(2,1)} %bitcast.10, bf16[2,384,5120]{2,1,0:T(8,128)(2,1)} %bitcast.11, bf16[2,32,5120]{2,1,0:T(8,128)(2,1)} %bitcast.13), custom_call_target="tpu_custom_call" | custom-call | bytes 4194304 | tf_op jit(solution)/shard_map/left_product/pallas_call | solution.py:274
  7.2 21.8 %all_to_all.15.parts_ref = bf16[16,64,384]{2,1,0:T(8,128)(2,1)S(1)} all-to-all(bf16[16,64,384]{2,1,0:T(8,128)(2,1)S(1)} %get-tuple-element.15), channel_id=1, replica_groups=mesh['dp'=16,'tensor'=8] {'dp'}, dimensions={0} | all-to-all | bytes 1572864 | tf_op jit(solution)/shard_map/all_to_all | solution.py:287
  29.0 1.1 %right_product_other.1 = (bf16[64,24,128]{2,1,0:T(8,128)(2,1)S(1)}, f32[64,384]{1,0:T(8,128)S(1)}, f32[8,128]{1,0:T(8,128)S(1)}) custom-call(bf16[16,64,384]{2,1,0:T(8,128)(2,1)S(1)} %all_to_all.15.parts_ref, bf16[2,384,5120]{2,1,0:T(8,128)(2,1)S(1)} %get-tuple-element.16.corrected_ref), custom_call_target="tpu_custom_call" | custom-call | flops 125829120 | bytes 4194304 | tf_op jit(solution)/shard_map/right_product_other/pallas_call | solution.py:293
  30.1 1.8 %collective-permute-start = (bf16[64,24,128]{2,1,0:T(8,128)(2,1)S(1)}, bf16[64,24,128]{2,1,0:T(8,128)(2,1)S(1)}, u32[]{:S(2)}, u32[]{:S(2)}) collective-permute-start(bf16[64,24,128]{2,1,0:T(8,128)(2,1)S(1)} %get-tuple-element.18), channel_id=1, source_target_pairs={{0,1},{1,0},{2,3},{3,2},{4,5},{5,4},{6,7},{7,6},{8,9},{9,8},{10,11... | collective-permute-start | bytes 1179656 | tf_op jit(solution)/shard_map/ppermute | solution.py:301
  31.9 0.9 %right_product_own.1.own_ref = f32[64,24,128]{2,1,0:T(8,128)S(1)} custom-call(f32[64,384]{1,0:T(8,128)S(1)} %get-tuple-element.17.summed_ref, bf16[2,384,5120]{2,1,0:T(8,128)(2,1)S(1)} %get-tuple-element.16.corrected_ref), custom_call_target="tpu_custom_call" | custom-call | flops 125829120 | bytes 4194304 | tf_op jit(solution)/shard_map/right_product_own/pallas_call | solution.py:302
  32.8 0.4 collective-permute-done.other_ref
  33.3 0.1 pair_sum.1
  33.3 17.7 %all_to_all.16.parts_ref = bf16[64,24,128]{2,1,0:T(8,128)(2,1)S(1)} all-to-all(bf16[64,24,128]{2,1,0:T(8,128)(2,1)S(1)} %pair_sum.1), channel_id=1, replica_groups={{0,2,4,6,8,10,12,14,16,18,20,22,24,26,28,30,32,34,36,38,40,42,44,46,48,..., dimensions={0} | all-to-all | bytes 786432 | tf_op jit(solution)/shard_map/all_to_all | solution.py:312
  51.0 4.0 %factor.1 = (bf16[64,24,128]{2,1,0:T(8,128)(2,1)S(1)}, f32[64,384]{1,0:T(8,128)}, bf16[2,768,128]{2,1,0:T(8,128)(2,1)S(1)}) custom-call(bf16[64,24,128]{2,1,0:T(8,128)(2,1)S(1)} %all_to_all.16.parts_ref, f32[64,384]{1,0:T(8,128)S(1)} %get-tuple-element.17.summed_ref), custom_call_target="tpu_custom_call" | custom-call | bytes 4194304 | tf_op jit(solution)/shard_map/factor/pallas_call | solution.py:314
  55.0 14.5 %all_to_all.17.right_ref = bf16[64,24,128]{2,1,0:T(8,128)(2,1)S(1)} all-to-all(bf16[64,24,128]{2,1,0:T(8,128)(2,1)S(1)} %get-tuple-element.20), channel_id=1, replica_groups={{0,2,4,6,8,10,12,14,16,18,20,22,24,26,28,30,32,34,36,38,40,42,44,46,48,..., dimensions={0} | all-to-all | bytes 786432 | tf_op jit(solution)/shard_map/all_to_all | solution.py:322
  69.6 3.2 %collective-permute-start.1 = (bf16[64,24,128]{2,1,0:T(8,128)(2,1)S(1)}, bf16[64,24,128]{2,1,0:T(8,128)(2,1)S(1)}, u32[]{:S(2)}, u32[]{:S(2)}) collective-permute-start(bf16[64,24,128]{2,1,0:T(8,128)(2,1)S(1)} %all_to_all.17.right_ref), channel_id=1, source_target_pairs={{0,1},{1,0},{2,3},{3,2},{4,5},{5,4},{6,7},{7,6},{8,9},{9,8},{10,11... | collective-permute-start | bytes 1179656 | tf_op jit(solution)/shard_map/ppermute | solution.py:324
  72.8 2.4 %new_error_own.1 = (bf16[2,384,5120]{2,1,0:T(8,128)(2,1)}, f32[64,40]{1,0:T(8,128)S(1)}) custom-call(bf16[64,24,128]{2,1,0:T(8,128)(2,1)S(1)} %all_to_all.17.right_ref, bf16[2,768,128]{2,1,0:T(8,128)(2,1)S(1)} %get-tuple-element.21.left_ref, bf16[2,384,5120]{2,1,0:T(8,128)(2,1)S(1)} %get-tuple-element.16.corrected_ref), custom_call_target="tpu_custom_call" | custom-call | flops 125829120 | bytes 4194304 | tf_op jit(solution)/shard_map/new_error_own/pallas_call | solution.py:332
  75.2 0.0 collective-permute-done.1.right_ref
  75.2 3.0 %new_error_other.1 = (bf16[2,384,5120]{2,1,0:T(8,128)(2,1)}, f32[64,40]{1,0:T(8,128)}) custom-call(bf16[64,24,128]{2,1,0:T(8,128)(2,1)S(1)} %collective-permute-done.1.right_ref, bf16[2,768,128]{2,1,0:T(8,128)(2,1)S(1)} %get-tuple-element.21.left_ref, bf16[2,384,5120]{2,1,0:T(8,128)(2,1)S(1)} %get-tuple-element.16.corrected_ref, ...), custom_call_target="tpu_custom_call", output_to_operand_aliasing={{0}: (4, {})} | custom-call | flops 125829120 | bytes 4194304 | tf_op jit(solution)/shard_map/new_error_other/pallas_call | solution.py:341
Async XLA Ops:
  30.1 3.1 %collective-permute-start = (bf16[64,24,128]{2,1,0:T(8,128)(2,1)S(1)}, bf16[64,24,128]{2,1,0:T(8,128)(2,1)S(1)}, u32[]{:S(2)}, u32[]{:S(2)}) collective-permute-start(bf16[64,24,128]{2,1,0:T(8,128)(2,1)S(1)} %get-tuple-element.18), channel_id=1, source_target_pairs={{0,1},{1,0},{2,3},{3,2},{4,5},{5,4},{6,7},{7,6},{8,9},{9,8},{10,11... | collective-permute-start | bytes 1179656 | tf_op jit(solution)/shard_map/ppermute | solution.py:301
  69.6 5.7 %collective-permute-start.1 = (bf16[64,24,128]{2,1,0:T(8,128)(2,1)S(1)}, bf16[64,24,128]{2,1,0:T(8,128)(2,1)S(1)}, u32[]{:S(2)}, u32[]{:S(2)}) collective-permute-start(bf16[64,24,128]{2,1,0:T(8,128)(2,1)S(1)} %all_to_all.17.right_ref), channel_id=1, source_target_pairs={{0,1},{1,0},{2,3},{3,2},{4,5},{5,4},{6,7},{7,6},{8,9},{9,8},{10,11... | collective-permute-start | bytes 1179656 | tf_op jit(solution)/shard_map/ppermute | solution.py:324

commit v3 on v2

--- a/solution.py
+++ b/solution.py
@@ -25,9 +25,13 @@
 CHUNK = 24
 STEP = 512
 TILE = 256
+BLOCK = 16
+PIECES = [(0, 0, 640), (0, 640, 640), (1, 0, 640), (1, 640, 640)]
+DP_ORDER = [10, 15, 14, 13, 12, 11, 9, 8, 7, 6, 5, 4, 3, 2, 1, 0]
+X_ORDER = [2, 3, 1, 0]
 BOTH_AXES = ("dp", "tensor")
 CORE_PAIRS = [(i, i ^ 1) for i in range(TENSOR)]
-SAME_CORE = [[i for i in range(DEVICES) if i % 2 == core] for core in range(2)]
+SAME_CORE = [[TENSOR * r + 2 * x + core for r in DP_ORDER for x in X_ORDER] for core in range(2)]
 
 
 def columns_at(start, size):
@@ -146,11 +150,20 @@
     ]
     shift = 1e-05 * jnp.where(first, trace[0], trace[1]) / RANK
     work = square + jnp.where(lane < BOTH, shift * eye, eye)
-    for j in range(RANK - 1):
-        column = jnp.where(first, work[:, j : j + 1], work[:, RANK + j : RANK + j + 1])
-        pivot_row = work[j : j + 1, :]
-        scaled = pivot_row / column[j : j + 1, :]
-        work = work - jnp.where(row > j, column, 0.0) * scaled
+    for start in range(0, RANK, BLOCK):
+        columns = [jnp.where(first, work[:, j : j + 1], work[:, RANK + j : RANK + j + 1]) for j in range(start, start + BLOCK)]
+        rows = [work[j : j + 1, :] for j in range(start, start + BLOCK)]
+        update = jnp.zeros_like(work)
+        for a in range(BLOCK):
+            inverse_pivot = 1.0 / columns[a][start + a : start + a + 1, :]
+            scaled = rows[a] * inverse_pivot
+            below = jnp.where(row > start + a, columns[a], 0.0)
+            update = update + below * scaled
+            for b in range(a + 1, BLOCK):
+                value = columns[a][start + b : start + b + 1, :]
+                rows[b] = rows[b] - value * scaled
+                columns[b] = columns[b] - below * (value * inverse_pivot)
+        work = work - update
     pivots = work * eye
     pivot = [
         jnp.sum(jnp.where(lane // RANK == m, pivots, 0.0), axis=1, keepdims=True) for m in range(MATS)
@@ -160,10 +173,10 @@
 
 def factor_kernel(parts_ref, summed_ref, out_ref, p_ref, left_ref, gram_ref):
     total = jnp.zeros((CHUNK, LANES), F32)
-    for r in range(DP):
-        block = parts_ref[CHIPS_X * r].astype(F32)
+    for i, r in enumerate(DP_ORDER):
+        block = parts_ref[CHIPS_X * i].astype(F32)
         for x in range(1, CHIPS_X):
-            block = block + parts_ref[CHIPS_X * r + x].astype(F32)
+            block = block + parts_ref[CHIPS_X * i + x].astype(F32)
         total = total + block
         gram_ref[r : r + 1, :] = block[20:21] + block[21:22] + block[22:23]
     gram = gram_ref[...]
@@ -206,22 +219,19 @@
     turned_ref[...] = wide_ref[:QUARTER, :].astype(BF16)
 
     copies = []
-    for i in range(QUARTER // TILE):
-        for g in range(2):
-            columns = columns_at(HALF * core + QUARTER * g + TILE * i, TILE)
-            local_columns = pl.ds(QUARTER * g + TILE * i, TILE)
-            rebuilt = lax.dot_general(
-                left_ref[g], turned_ref[TILE * i : TILE * i + TILE, :], NT, preferred_element_type=F32
-            )
-            for m in range(MATS):
-                stage_ref[m, :, local_columns] = (
-                    corrected_ref[m, :, columns].astype(F32) - rebuilt[ROWS * m : ROWS * m + ROWS]
-                ).astype(BF16)
-            copy = pltpu.make_async_copy(
-                stage_ref.at[:, :, local_columns], out_ref.at[:, :, columns], sems.at[i, g]
-            )
-            copy.start()
-            copies.append(copy)
+    for n, (g, first, size) in enumerate(PIECES):
+        columns = pl.ds(pl.multiple_of(HALF * core + QUARTER * g + first, LANES), size)
+        local_columns = pl.ds(QUARTER * g + first, size)
+        rebuilt = lax.dot_general(
+            left_ref[g], turned_ref[first : first + size, :], NT, preferred_element_type=F32
+        )
+        for m in range(MATS):
+            stage_ref[m, :, local_columns] = (
+                corrected_ref[m, :, columns].astype(F32) - rebuilt[ROWS * m : ROWS * m + ROWS]
+            ).astype(BF16)
+        copy = pltpu.make_async_copy(stage_ref.at[:, :, local_columns], out_ref.at[:, :, columns], sems.at[n])
+        copy.start()
+        copies.append(copy)
 
     me = lax.axis_index("dp") * TENSOR + lax.axis_index("tensor")
     wide_ref[QUARTER:, :] = jnp.zeros((LANES, LANES), F32)
@@ -284,7 +294,7 @@
         ],
     )(in_hbm(grad[0]), in_hbm(error[0]), in_hbm(q_init.transpose(1, 2, 0)))
 
-    parts = lax.all_to_all(part, "dp", 0, 0, tiled=True)
+    parts = lax.all_to_all(part, "dp", 0, 0, axis_index_groups=[DP_ORDER], tiled=True)
 
     turned = pltpu.VMEM((QUARTER, LANES), F32)
     tail = pltpu.VMEM((CHIPS, 8, LANES), F32)
@@ -326,7 +336,7 @@
         pltpu.VMEM((QUARTER + LANES, LANES), F32),
         pltpu.VMEM((QUARTER, LANES), BF16),
         pltpu.VMEM((MATS, ROWS, HALF), BF16),
-        pltpu.SemaphoreType.DMA((QUARTER // TILE, 2)),
+        pltpu.SemaphoreType.DMA((len(PIECES),)),
     ]
     error_shape = jax.ShapeDtypeStruct((MATS, ROWS, WIDTH), BF16)
     new_error, q_factor = call(

time: 78.5 us -> 71.4 us (0.910)
  blocking collectives: 54 us -> 49.1 us
  Pallas kernels: 18.2 us -> 16.3 us
    all_to_all x1, blocking collectives: 21.8 us -> 19.2 us  [local(): lax.all_to_all(part, 'dp', 0, 0, axis_index_groups=[DP_ORDER], tiled=True)]
    pallas_call x1, Pallas kernels: 4.02 us -> 2.05 us  [local(): call(factor_kernel, 'factor', [WHOLE] * 2, [chunks, jax.ShapeDtypeStruct(...]
    all_to_all x1, blocking collectives: 17.7 us -> 15.9 us  [local(): lax.all_to_all(partial_q, BOTH_AXES, 0, 0, axis_index_groups=SAME_CORE, t...]
  transfers between devices with their start and end apart: 2 -> 2, of which waited for: 1 -> 1; matrix products, arithmetic and copies ran while one was open for 0% -> 0% of each run, Pallas kernels for 4% -> 5%
where the time goes in v3:
time: 71.4 us; the launch traced here: 71.1 us
  blocking collectives  49.1 us (69%)
  Pallas kernels  16.3 us (23%)
  starting transfers between devices  4.66 us (7%)
    all_to_all x1, blocking collectives, local(): lax.all_to_all(part, 'dp', 0, 0, axis_index_groups=[DP_ORDER], tiled=True)  19.2 us
    all_to_all x1, blocking collectives, local(): lax.all_to_all(partial_q, BOTH_AXES, 0, 0, axis_index_groups=SAME_CORE, t...  15.9 us
    all_to_all x1, blocking collectives, local(): lax.all_to_all(q_own, BOTH_AXES, 0, 0, axis_index_groups=SAME_CORE, tiled...  14 us
    pallas_call x1, Pallas kernels, local(): call(left_kernel, 'left_product', [IN_HBM] * 3, [pltpu.VMEM((MATS, ROWS,...  6.59 us
    pallas_call x1, Pallas kernels, local(): call(other_error_kernel, 'new_error_other', [WHOLE] * 4 + [IN_HBM], [erro...  3.09 us
    ppermute x1, starting transfers between devices, local(): q_other = lax.ppermute(q_half, 'tensor', CORE_PAIRS)  3.06 us
    pallas_call x1, Pallas kernels, local(): call(own_error_kernel, 'new_error_own', [WHOLE] * 3, [error_shape, pltpu....  2.47 us
    pallas_call x1, Pallas kernels, local(): call(factor_kernel, 'factor', [WHOLE] * 2, [chunks, jax.ShapeDtypeStruct(...  2.05 us
  transfers between devices with their start and end apart: 2, of which 1 were waited for; matrix products, arithmetic and copies ran while one was open for 0% of the time, Pallas kernels for 5%

profile of v3, /device:TPU:1, one launch (start us, length us, event | category | flops | bytes accessed | tf_op | source)
XLA Modules:
  0.0 71.1 jit_solution(13312136201421977792)
XLA Ops:
  0.6 6.6 %left_product.1 = (bf16[2,384,5120]{2,1,0:T(8,128)(2,1)S(1)}, bf16[16,64,384]{2,1,0:T(8,128)(2,1)S(1)}) custom-call(bf16[2,384,5120]{2,1,0:T(8,128)(2,1)} %bitcast.10, bf16[2,384,5120]{2,1,0:T(8,128)(2,1)} %bitcast.11, bf16[2,32,5120]{2,1,0:T(8,128)(2,1)} %bitcast.13), custom_call_target="tpu_custom_call" | custom-call | bytes 4194304 | tf_op jit(solution)/shard_map/left_product/pallas_call | solution.py:284
  7.2 19.2 %all_to_all.15.parts_ref = bf16[16,64,384]{2,1,0:T(8,128)(2,1)S(1)} all-to-all(bf16[16,64,384]{2,1,0:T(8,128)(2,1)S(1)} %get-tuple-element.15), channel_id=1, replica_groups={{80,120,112,104,96,88,72,64,56,48,40,32,24,16,8,0},{81,121,113,105,97,8..., dimensions={0} | all-to-all | bytes 1572864 | tf_op jit(solution)/shard_map/all_to_all | solution.py:297
  26.5 1.1 %right_product_other.1 = (bf16[64,24,128]{2,1,0:T(8,128)(2,1)S(1)}, f32[64,384]{1,0:T(8,128)S(1)}, f32[8,128]{1,0:T(8,128)S(1)}) custom-call(bf16[16,64,384]{2,1,0:T(8,128)(2,1)S(1)} %all_to_all.15.parts_ref, bf16[2,384,5120]{2,1,0:T(8,128)(2,1)S(1)} %get-tuple-element.16.corrected_ref), custom_call_target="tpu_custom_call" | custom-call | flops 125829120 | bytes 4194304 | tf_op jit(solution)/shard_map/right_product_other/pallas_call | solution.py:303
  27.6 1.6 %collective-permute-start = (bf16[64,24,128]{2,1,0:T(8,128)(2,1)S(1)}, bf16[64,24,128]{2,1,0:T(8,128)(2,1)S(1)}, u32[]{:S(2)}, u32[]{:S(2)}) collective-permute-start(bf16[64,24,128]{2,1,0:T(8,128)(2,1)S(1)} %get-tuple-element.18), channel_id=1, source_target_pairs={{0,1},{1,0},{2,3},{3,2},{4,5},{5,4},{6,7},{7,6},{8,9},{9,8},{10,11... | collective-permute-start | bytes 1179656 | tf_op jit(solution)/shard_map/ppermute | solution.py:311
  29.2 0.9 %right_product_own.1.own_ref = f32[64,24,128]{2,1,0:T(8,128)S(1)} custom-call(f32[64,384]{1,0:T(8,128)S(1)} %get-tuple-element.17.summed_ref, bf16[2,384,5120]{2,1,0:T(8,128)(2,1)S(1)} %get-tuple-element.16.corrected_ref), custom_call_target="tpu_custom_call" | custom-call | flops 125829120 | bytes 4194304 | tf_op jit(solution)/shard_map/right_product_own/pallas_call | solution.py:312
  30.1 0.4 collective-permute-done.other_ref
  30.5 0.1 pair_sum.1
  30.6 15.9 %all_to_all.16.parts_ref = bf16[64,24,128]{2,1,0:T(8,128)(2,1)S(1)} all-to-all(bf16[64,24,128]{2,1,0:T(8,128)(2,1)S(1)} %pair_sum.1), channel_id=1, replica_groups={{84,86,82,80,124,126,122,120,116,118,114,112,108,110,106,104,100,102,98..., dimensions={0} | all-to-all | bytes 786432 | tf_op jit(solution)/shard_map/all_to_all | solution.py:322
  46.5 2.0 %factor.1 = (bf16[64,24,128]{2,1,0:T(8,128)(2,1)S(1)}, f32[64,384]{1,0:T(8,128)}, bf16[2,768,128]{2,1,0:T(8,128)(2,1)S(1)}) custom-call(bf16[64,24,128]{2,1,0:T(8,128)(2,1)S(1)} %all_to_all.16.parts_ref, f32[64,384]{1,0:T(8,128)S(1)} %get-tuple-element.17.summed_ref), custom_call_target="tpu_custom_call" | custom-call | bytes 4194304 | tf_op jit(solution)/shard_map/factor/pallas_call | solution.py:324
  48.5 14.0 %all_to_all.17.right_ref = bf16[64,24,128]{2,1,0:T(8,128)(2,1)S(1)} all-to-all(bf16[64,24,128]{2,1,0:T(8,128)(2,1)S(1)} %get-tuple-element.20), channel_id=1, replica_groups={{84,86,82,80,124,126,122,120,116,118,114,112,108,110,106,104,100,102,98..., dimensions={0} | all-to-all | bytes 786432 | tf_op jit(solution)/shard_map/all_to_all | solution.py:332
  62.5 3.1 %collective-permute-start.1 = (bf16[64,24,128]{2,1,0:T(8,128)(2,1)S(1)}, bf16[64,24,128]{2,1,0:T(8,128)(2,1)S(1)}, u32[]{:S(2)}, u32[]{:S(2)}) collective-permute-start(bf16[64,24,128]{2,1,0:T(8,128)(2,1)S(1)} %all_to_all.17.right_ref), channel_id=1, source_target_pairs={{0,1},{1,0},{2,3},{3,2},{4,5},{5,4},{6,7},{7,6},{8,9},{9,8},{10,11... | collective-permute-start | bytes 1179656 | tf_op jit(solution)/shard_map/ppermute | solution.py:334
  65.6 2.5 %new_error_own.1 = (bf16[2,384,5120]{2,1,0:T(8,128)(2,1)}, f32[64,40]{1,0:T(8,128)S(1)}) custom-call(bf16[64,24,128]{2,1,0:T(8,128)(2,1)S(1)} %all_to_all.17.right_ref, bf16[2,768,128]{2,1,0:T(8,128)(2,1)S(1)} %get-tuple-element.21.left_ref, bf16[2,384,5120]{2,1,0:T(8,128)(2,1)S(1)} %get-tuple-element.16.corrected_ref), custom_call_target="tpu_custom_call" | custom-call | flops 125829120 | bytes 4194304 | tf_op jit(solution)/shard_map/new_error_own/pallas_call | solution.py:342
  68.0 0.0 collective-permute-done.1.right_ref
  68.1 3.1 %new_error_other.1 = (bf16[2,384,5120]{2,1,0:T(8,128)(2,1)}, f32[64,40]{1,0:T(8,128)}) custom-call(bf16[64,24,128]{2,1,0:T(8,128)(2,1)S(1)} %collective-permute-done.1.right_ref, bf16[2,768,128]{2,1,0:T(8,128)(2,1)S(1)} %get-tuple-element.21.left_ref, bf16[2,384,5120]{2,1,0:T(8,128)(2,1)S(1)} %get-tuple-element.16.corrected_ref, ...), custom_call_target="tpu_custom_call", output_to_operand_aliasing={{0}: (4, {})} | custom-call | flops 125829120 | bytes 4194304 | tf_op jit(solution)/shard_map/new_error_other/pallas_call | solution.py:351
Async XLA Ops:
  27.6 2.9 %collective-permute-start = (bf16[64,24,128]{2,1,0:T(8,128)(2,1)S(1)}, bf16[64,24,128]{2,1,0:T(8,128)(2,1)S(1)}, u32[]{:S(2)}, u32[]{:S(2)}) collective-permute-start(bf16[64,24,128]{2,1,0:T(8,128)(2,1)S(1)} %get-tuple-element.18), channel_id=1, source_target_pairs={{0,1},{1,0},{2,3},{3,2},{4,5},{5,4},{6,7},{7,6},{8,9},{9,8},{10,11... | collective-permute-start | bytes 1179656 | tf_op jit(solution)/shard_map/ppermute | solution.py:311
  62.5 5.5 %collective-permute-start.1 = (bf16[64,24,128]{2,1,0:T(8,128)(2,1)S(1)}, bf16[64,24,128]{2,1,0:T(8,128)(2,1)S(1)}, u32[]{:S(2)}, u32[]{:S(2)}) collective-permute-start(bf16[64,24,128]{2,1,0:T(8,128)(2,1)S(1)} %all_to_all.17.right_ref), channel_id=1, source_target_pairs={{0,1},{1,0},{2,3},{3,2},{4,5},{5,4},{6,7},{7,6},{8,9},{9,8},{10,11... | collective-permute-start | bytes 1179656 | tf_op jit(solution)/shard_map/ppermute | solution.py:334

commit v4 on v3

--- a/solution.py
+++ b/solution.py
@@ -23,15 +23,20 @@
 SHARE = WIDTH // DEVICES
 HEAD = 16 * CHIPS
 CHUNK = 24
-STEP = 512
+READS = [1024] * 4 + [512, 256, 256]
 TILE = 256
 BLOCK = 16
 PIECES = [(0, 0, 640), (0, 640, 640), (1, 0, 640), (1, 640, 640)]
 DP_ORDER = [10, 15, 14, 13, 12, 11, 9, 8, 7, 6, 5, 4, 3, 2, 1, 0]
-X_ORDER = [2, 3, 1, 0]
+CHIP_ORDER = [
+    42, 52, 40, 44, 60, 63, 24, 54, 0, 11, 45, 56, 18, 34, 10, 55,
+    46, 38, 15, 31, 57, 61, 36, 5, 17, 62, 21, 22, 49, 6, 1, 29,
+    41, 33, 28, 30, 51, 8, 2, 26, 32, 48, 7, 27, 23, 25, 4, 39,
+    37, 14, 59, 19, 43, 16, 47, 20, 3, 53, 13, 50, 35, 9, 12, 58,
+]
 BOTH_AXES = ("dp", "tensor")
 CORE_PAIRS = [(i, i ^ 1) for i in range(TENSOR)]
-SAME_CORE = [[TENSOR * r + 2 * x + core for r in DP_ORDER for x in X_ORDER] for core in range(2)]
+SAME_CORE = [[2 * chip + core for chip in CHIP_ORDER] for core in range(2)]
 
 
 def columns_at(start, size):
@@ -39,10 +44,9 @@
 
 
 def left_kernel(grad_ref, error_ref, q_ref, corrected_ref, out_ref, error_vmem, q_vmem, acc_ref, sems):
-    starts = range(0, WIDTH, STEP)
+    reads = [pl.ds(sum(READS[:i]), size) for i, size in enumerate(READS)]
     copies = []
-    for i, start in enumerate(starts):
-        columns = pl.ds(start, STEP)
+    for i, columns in enumerate(reads):
         pairs = [(q_ref, q_vmem), (grad_ref, corrected_ref), (error_ref, error_vmem)]
         copies.append(
             [
@@ -52,8 +56,7 @@
         )
         for copy in copies[-1]:
             copy.start()
-    for i, start in enumerate(starts):
-        columns = pl.ds(start, STEP)
+    for i, columns in enumerate(reads):
         for copy in copies[i]:
             copy.wait()
         for m in range(MATS):
@@ -173,10 +176,11 @@
 
 def factor_kernel(parts_ref, summed_ref, out_ref, p_ref, left_ref, gram_ref):
     total = jnp.zeros((CHUNK, LANES), F32)
-    for i, r in enumerate(DP_ORDER):
-        block = parts_ref[CHIPS_X * i].astype(F32)
-        for x in range(1, CHIPS_X):
-            block = block + parts_ref[CHIPS_X * i + x].astype(F32)
+    for r in range(DP):
+        places = [CHIP_ORDER.index(CHIPS_X * r + x) for x in range(CHIPS_X)]
+        block = parts_ref[places[0]].astype(F32)
+        for place in places[1:]:
+            block = block + parts_ref[place].astype(F32)
         total = total + block
         gram_ref[r : r + 1, :] = block[20:21] + block[21:22] + block[22:23]
     gram = gram_ref[...]
@@ -209,7 +213,13 @@
             left_ref[g, ROWS * m : ROWS * m + ROWS, :] = jnp.where(lane // RANK == 2 * g + m, p, 0.0).astype(BF16)
 
 
-def half_error(right_ref, left_ref, corrected_ref, out_ref, core, wide_ref, turned_ref, stage_ref, sems):
+def piece_copy(stage, out_ref, core, piece, sem):
+    g, first, size = piece
+    columns = pl.ds(pl.multiple_of(HALF * core + QUARTER * g + first, LANES), size)
+    return pltpu.make_async_copy(stage, out_ref.at[:, :, columns], sem)
+
+
+def half_error(right_ref, left_ref, corrected_ref, out_ref, core, wide_ref, turned_ref, stage_ref, sems, rest_ref=None):
     for n in range(CHIPS // 16):
         block = right_ref[16 * n : 16 * n + 16].astype(F32)
         wide_ref[256 * n : 256 * n + 256, :] = block[:, 0:16].reshape(256, LANES)
@@ -221,40 +231,54 @@
     copies = []
     for n, (g, first, size) in enumerate(PIECES):
         columns = pl.ds(pl.multiple_of(HALF * core + QUARTER * g + first, LANES), size)
-        local_columns = pl.ds(QUARTER * g + first, size)
         rebuilt = lax.dot_general(
             left_ref[g], turned_ref[first : first + size, :], NT, preferred_element_type=F32
         )
+        keep = rest_ref is not None and n == len(PIECES) - 1
+        stage = rest_ref if keep else stage_ref.at[:, :, pl.ds(QUARTER * g + first, size)]
         for m in range(MATS):
-            stage_ref[m, :, local_columns] = (
+            stage[m] = (
                 corrected_ref[m, :, columns].astype(F32) - rebuilt[ROWS * m : ROWS * m + ROWS]
             ).astype(BF16)
-        copy = pltpu.make_async_copy(stage_ref.at[:, :, local_columns], out_ref.at[:, :, columns], sems.at[n])
-        copy.start()
-        copies.append(copy)
+        if not keep:
+            copies.append(piece_copy(stage, out_ref, core, PIECES[n], sems.at[n]))
+            copies[-1].start()
 
     me = lax.axis_index("dp") * TENSOR + lax.axis_index("tensor")
     wide_ref[QUARTER:, :] = jnp.zeros((LANES, LANES), F32)
     start = pl.multiple_of(SHARE * (me % (DEVICES // 4)), 8)
     own = wide_ref[pl.ds(start, LANES), :].T
     upper = (me // (DEVICES // 4)) % 2 == 1
-    own = jnp.where(upper, own[BOTH:, :SHARE], own[:BOTH, :SHARE])
-    for copy in copies:
+    return copies, jnp.where(upper, own[BOTH:, :SHARE], own[:BOTH, :SHARE])
+
+
+def own_error_kernel(
+    right_ref, left_ref, corrected_ref, p_ref, out_ref, q_ref, rest_ref, p_out_ref, *scratch
+):
+    *scratch, p_sem = scratch
+    p_copy = pltpu.make_async_copy(p_ref, p_out_ref, p_sem)
+    p_copy.start()
+    core = lax.axis_index("tensor") % 2
+    copies, q_ref[...] = half_error(right_ref, left_ref, corrected_ref, out_ref, core, *scratch, rest_ref)
+    for copy in [*copies, p_copy]:
         copy.wait()
-    return own, me // CHIPS == core
-
-
-def own_error_kernel(right_ref, left_ref, corrected_ref, out_ref, q_ref, *scratch):
+
+
+def other_error_kernel(
+    right_ref, left_ref, corrected_ref, q_own_ref, rest_ref, error_ref, out_ref, q_out_ref, *scratch
+):
+    del error_ref
+    *scratch, q_ref, rest_sem, q_sem = scratch
     core = lax.axis_index("tensor") % 2
-    own, _ = half_error(right_ref, left_ref, corrected_ref, out_ref, core, *scratch)
-    q_ref[...] = own
-
-
-def other_error_kernel(right_ref, left_ref, corrected_ref, q_own_ref, error_ref, out_ref, q_ref, *scratch):
-    del error_ref
-    core = 1 - lax.axis_index("tensor") % 2
-    own, here = half_error(right_ref, left_ref, corrected_ref, out_ref, core, *scratch)
-    q_ref[...] = jnp.where(here, own, q_own_ref[...])
+    rest_copy = piece_copy(rest_ref, out_ref, core, PIECES[-1], rest_sem)
+    rest_copy.start()
+    copies, other = half_error(right_ref, left_ref, corrected_ref, out_ref, 1 - core, *scratch)
+    me = lax.axis_index("dp") * TENSOR + lax.axis_index("tensor")
+    q_ref[...] = jnp.where(me // CHIPS == core, q_own_ref[...], other)
+    q_copy = pltpu.make_async_copy(q_ref, q_out_ref, q_sem)
+    q_copy.start()
+    for copy in [rest_copy, *copies, q_copy]:
+        copy.wait()
 
 
 WHOLE = pl.BlockSpec(memory_space=pltpu.VMEM)
@@ -280,7 +304,6 @@
 
 
 def local(grad, error, q_init):
-    steps = WIDTH // STEP
     corrected, part = call(
         left_kernel,
         "left_product",
@@ -290,7 +313,7 @@
             pltpu.VMEM((MATS, ROWS, WIDTH), BF16),
             pltpu.VMEM((MATS, RANK, WIDTH), BF16),
             pltpu.VMEM((MATS, ROWS, RANK), F32),
-            pltpu.SemaphoreType.DMA((3, steps)),
+            pltpu.SemaphoreType.DMA((3, len(READS))),
         ],
     )(in_hbm(grad[0]), in_hbm(error[0]), in_hbm(q_init.transpose(1, 2, 0)))
 
@@ -325,7 +348,7 @@
         factor_kernel,
         "factor",
         [WHOLE] * 2,
-        [chunks, jax.ShapeDtypeStruct((BOTH, ROWS), F32), pltpu.VMEM((2, MATS * ROWS, LANES), BF16)],
+        [chunks, pltpu.VMEM((BOTH, ROWS), F32), pltpu.VMEM((2, MATS * ROWS, LANES), BF16)],
         scratch=[pltpu.VMEM((16, LANES), F32)],
     )(partial_q, summed)
 
@@ -339,29 +362,31 @@
         pltpu.SemaphoreType.DMA((len(PIECES),)),
     ]
     error_shape = jax.ShapeDtypeStruct((MATS, ROWS, WIDTH), BF16)
-    new_error, q_factor = call(
+    factor_shape = jax.ShapeDtypeStruct((BOTH, ROWS), F32)
+    rest_shape = pltpu.VMEM((MATS, ROWS, PIECES[-1][2]), BF16)
+    new_error, q_factor, rest, p_factor = call(
         own_error_kernel,
         "new_error_own",
-        [WHOLE] * 3,
-        [error_shape, pltpu.VMEM((BOTH, SHARE), F32)],
-        [IN_HBM, WHOLE],
-        scratch=scratch,
+        [WHOLE] * 4,
+        [error_shape, pltpu.VMEM((BOTH, SHARE), F32), rest_shape, factor_shape],
+        [IN_HBM, WHOLE, WHOLE, IN_HBM],
+        scratch=[*scratch, pltpu.SemaphoreType.DMA],
         flops=half_flops,
-    )(q_half, left, corrected)
+    )(q_half, left, corrected, p_turned)
     new_error, q_factor = call(
         other_error_kernel,
         "new_error_other",
-        [WHOLE] * 4 + [IN_HBM],
+        [WHOLE] * 5 + [IN_HBM],
         [error_shape, jax.ShapeDtypeStruct((BOTH, SHARE), F32)],
-        [IN_HBM, WHOLE],
-        scratch=scratch,
+        [IN_HBM, IN_HBM],
+        scratch=[*scratch, pltpu.VMEM((BOTH, SHARE), F32), pltpu.SemaphoreType.DMA, pltpu.SemaphoreType.DMA],
         flops=half_flops,
-        input_output_aliases={4: 0},
-    )(q_other, left, corrected, q_factor, new_error)
+        input_output_aliases={5: 0},
+    )(q_other, left, corrected, q_factor, rest, new_error)
 
     return (
         new_error[None],
-        p_turned.reshape(MATS, RANK, ROWS).transpose(0, 2, 1),
+        p_factor.reshape(MATS, RANK, ROWS).transpose(0, 2, 1),
         q_factor.reshape(MATS, RANK, SHARE).transpose(2, 0, 1),
     )
 

time: 71.4 us -> 69.4 us (0.972)
  Pallas kernels: 16.3 us -> 15 us
    pallas_call x3, Pallas kernels: 7.61 us -> 6.25 us  [the longest x1 2.49 us: local(): call(other_error_kernel, 'new_error_other', [WHOLE] * 5 + [IN_HBM], [erro...]
  transfers between devices with their start and end apart: 2 -> 2, of which waited for: 1 -> 1; matrix products, arithmetic and copies ran while one was open for 0% -> 0% of each run, Pallas kernels for 5% -> 4%
where the time goes in v4:
time: 69.4 us; the launch traced here: 69.2 us
  blocking collectives  49.1 us (71%)
  Pallas kernels  15 us (22%)
  starting transfers between devices  3.98 us (6%)
    all_to_all x1, blocking collectives, local(): lax.all_to_all(part, 'dp', 0, 0, axis_index_groups=[DP_ORDER], tiled=True)  19.2 us
    all_to_all x1, blocking collectives, local(): lax.all_to_all(partial_q, BOTH_AXES, 0, 0, axis_index_groups=SAME_CORE, t...  16 us
    all_to_all x1, blocking collectives, local(): lax.all_to_all(q_own, BOTH_AXES, 0, 0, axis_index_groups=SAME_CORE, tiled...  13.9 us
    pallas_call x1, Pallas kernels, local(): call(left_kernel, 'left_product', [IN_HBM] * 3, [pltpu.VMEM((MATS, ROWS,...  6.66 us
    pallas_call x1, Pallas kernels, local(): call(other_error_kernel, 'new_error_other', [WHOLE] * 5 + [IN_HBM], [erro...  2.49 us
    ppermute x1, starting transfers between devices, local(): q_other = lax.ppermute(q_half, 'tensor', CORE_PAIRS)  2.38 us
    pallas_call x1, Pallas kernels, local(): call(own_error_kernel, 'new_error_own', [WHOLE] * 4, [error_shape, pltpu....  2.19 us
    ppermute x1, starting transfers between devices, local(): from_other = lax.ppermute(for_other, 'tensor', CORE_PAIRS)  1.61 us
  transfers between devices with their start and end apart: 2, of which 1 were waited for; matrix products, arithmetic and copies ran while one was open for 0% of the time, Pallas kernels for 4%

profile of v4, /device:TPU:1, one launch (start us, length us, event | category | flops | bytes accessed | tf_op | source)
XLA Modules:
  0.0 69.2 jit_solution(2906836307283014819)
XLA Ops:
  0.6 6.7 %left_product.1 = (bf16[2,384,5120]{2,1,0:T(8,128)(2,1)S(1)}, bf16[16,64,384]{2,1,0:T(8,128)(2,1)S(1)}) custom-call(bf16[2,384,5120]{2,1,0:T(8,128)(2,1)} %bitcast.10, bf16[2,384,5120]{2,1,0:T(8,128)(2,1)} %bitcast.11, bf16[2,32,5120]{2,1,0:T(8,128)(2,1)} %bitcast.13), custom_call_target="tpu_custom_call" | custom-call | bytes 4194304 | tf_op jit(solution)/shard_map/left_product/pallas_call | solution.py:307
  7.3 19.2 %all_to_all.15.parts_ref = bf16[16,64,384]{2,1,0:T(8,128)(2,1)S(1)} all-to-all(bf16[16,64,384]{2,1,0:T(8,128)(2,1)S(1)} %get-tuple-element.17), channel_id=1, replica_groups={{80,120,112,104,96,88,72,64,56,48,40,32,24,16,8,0},{81,121,113,105,97,8..., dimensions={0} | all-to-all | bytes 1572864 | tf_op jit(solution)/shard_map/all_to_all | solution.py:320
  26.5 1.1 %right_product_other.1 = (bf16[64,24,128]{2,1,0:T(8,128)(2,1)S(1)}, f32[64,384]{1,0:T(8,128)S(1)}, f32[8,128]{1,0:T(8,128)S(1)}) custom-call(bf16[16,64,384]{2,1,0:T(8,128)(2,1)S(1)} %all_to_all.15.parts_ref, bf16[2,384,5120]{2,1,0:T(8,128)(2,1)S(1)} %get-tuple-element.18.corrected_ref), custom_call_target="tpu_custom_call" | custom-call | flops 125829120 | bytes 4194304 | tf_op jit(solution)/shard_map/right_product_other/pallas_call | solution.py:326
  27.7 1.6 %collective-permute-start = (bf16[64,24,128]{2,1,0:T(8,128)(2,1)S(1)}, bf16[64,24,128]{2,1,0:T(8,128)(2,1)S(1)}, u32[]{:S(2)}, u32[]{:S(2)}) collective-permute-start(bf16[64,24,128]{2,1,0:T(8,128)(2,1)S(1)} %get-tuple-element.20), channel_id=1, source_target_pairs={{0,1},{1,0},{2,3},{3,2},{4,5},{5,4},{6,7},{7,6},{8,9},{9,8},{10,11... | collective-permute-start | bytes 1179656 | tf_op jit(solution)/shard_map/ppermute | solution.py:334
  29.3 0.9 %right_product_own.1.own_ref = f32[64,24,128]{2,1,0:T(8,128)S(1)} custom-call(f32[64,384]{1,0:T(8,128)S(1)} %get-tuple-element.19.summed_ref, bf16[2,384,5120]{2,1,0:T(8,128)(2,1)S(1)} %get-tuple-element.18.corrected_ref), custom_call_target="tpu_custom_call" | custom-call | flops 125829120 | bytes 4194304 | tf_op jit(solution)/shard_map/right_product_own/pallas_call | solution.py:335
  30.2 0.4 collective-permute-done.other_ref
  30.6 0.1 pair_sum.1
  30.7 16.0 %all_to_all.16.parts_ref = bf16[64,24,128]{2,1,0:T(8,128)(2,1)S(1)} all-to-all(bf16[64,24,128]{2,1,0:T(8,128)(2,1)S(1)} %pair_sum.1), channel_id=1, replica_groups={{84,104,80,88,120,126,48,108,0,22,90,112,36,68,20,110,92,76,30,62,114,1..., dimensions={0} | all-to-all | bytes 786432 | tf_op jit(solution)/shard_map/all_to_all | solution.py:345
  46.7 1.6 %factor.1 = (bf16[64,24,128]{2,1,0:T(8,128)(2,1)S(1)}, f32[64,384]{1,0:T(8,128)S(1)}, bf16[2,768,128]{2,1,0:T(8,128)(2,1)S(1)}) custom-call(bf16[64,24,128]{2,1,0:T(8,128)(2,1)S(1)} %all_to_all.16.parts_ref, f32[64,384]{1,0:T(8,128)S(1)} %get-tuple-element.19.summed_ref), custom_call_target="tpu_custom_call" | custom-call | bytes 4194304 | tf_op jit(solution)/shard_map/factor/pallas_call | solution.py:347
  48.3 13.9 %all_to_all.17.right_ref = bf16[64,24,128]{2,1,0:T(8,128)(2,1)S(1)} all-to-all(bf16[64,24,128]{2,1,0:T(8,128)(2,1)S(1)} %get-tuple-element.22), channel_id=1, replica_groups={{84,104,80,88,120,126,48,108,0,22,90,112,36,68,20,110,92,76,30,62,114,1..., dimensions={0} | all-to-all | bytes 786432 | tf_op jit(solution)/shard_map/all_to_all | solution.py:355
  62.1 2.4 %collective-permute-start.1 = (bf16[64,24,128]{2,1,0:T(8,128)(2,1)S(1)}, bf16[64,24,128]{2,1,0:T(8,128)(2,1)S(1)}, u32[]{:S(2)}, u32[]{:S(2)}) collective-permute-start(bf16[64,24,128]{2,1,0:T(8,128)(2,1)S(1)} %all_to_all.17.right_ref), channel_id=1, source_target_pairs={{0,1},{1,0},{2,3},{3,2},{4,5},{5,4},{6,7},{7,6},{8,9},{9,8},{10,11... | collective-permute-start | bytes 1179656 | tf_op jit(solution)/shard_map/ppermute | solution.py:357
  64.5 2.2 %new_error_own.1 = (bf16[2,384,5120]{2,1,0:T(8,128)(2,1)}, f32[64,40]{1,0:T(8,128)S(1)}, bf16[2,384,640]{2,1,0:T(8,128)(2,1)S(1)}, f32[64,384]{1,0:T(8,128)}) custom-call(bf16[64,24,128]{2,1,0:T(8,128)(2,1)S(1)} %all_to_all.17.right_ref, bf16[2,768,128]{2,1,0:T(8,128)(2,1)S(1)} %get-tuple-element.23.left_ref, ...), custom_call_target="tpu_custom_call" | custom-call | flops 125829120 | bytes 4194304 | tf_op jit(solution)/shard_map/new_error_own/pallas_call | solution.py:367
  66.7 0.0 collective-permute-done.1.right_ref
  66.7 2.5 %new_error_other.1 = (bf16[2,384,5120]{2,1,0:T(8,128)(2,1)}, f32[64,40]{1,0:T(8,128)}) custom-call(bf16[64,24,128]{2,1,0:T(8,128)(2,1)S(1)} %collective-permute-done.1.right_ref, bf16[2,768,128]{2,1,0:T(8,128)(2,1)S(1)} %get-tuple-element.23.left_ref, bf16[2,384,5120]{2,1,0:T(8,128)(2,1)S(1)} %get-tuple-element.18.corrected_ref, ...), custom_call_target="tpu_custom_call", output_to_operand_aliasing={{0}: (5, {})} | custom-call | flops 125829120 | bytes 4194304 | tf_op jit(solution)/shard_map/new_error_other/pallas_call | solution.py:376
Async XLA Ops:
  27.7 3.0 %collective-permute-start = (bf16[64,24,128]{2,1,0:T(8,128)(2,1)S(1)}, bf16[64,24,128]{2,1,0:T(8,128)(2,1)S(1)}, u32[]{:S(2)}, u32[]{:S(2)}) collective-permute-start(bf16[64,24,128]{2,1,0:T(8,128)(2,1)S(1)} %get-tuple-element.20), channel_id=1, source_target_pairs={{0,1},{1,0},{2,3},{3,2},{4,5},{5,4},{6,7},{7,6},{8,9},{9,8},{10,11... | collective-permute-start | bytes 1179656 | tf_op jit(solution)/shard_map/ppermute | solution.py:334
  62.1 4.6 %collective-permute-start.1 = (bf16[64,24,128]{2,1,0:T(8,128)(2,1)S(1)}, bf16[64,24,128]{2,1,0:T(8,128)(2,1)S(1)}, u32[]{:S(2)}, u32[]{:S(2)}) collective-permute-start(bf16[64,24,128]{2,1,0:T(8,128)(2,1)S(1)} %all_to_all.17.right_ref), channel_id=1, source_target_pairs={{0,1},{1,0},{2,3},{3,2},{4,5},{5,4},{6,7},{7,6},{8,9},{9,8},{10,11... | collective-permute-start | bytes 1179656 | tf_op jit(solution)/shard_map/ppermute | solution.py:357

commit v5 on v4

--- a/solution.py
+++ b/solution.py
@@ -23,11 +23,11 @@
 SHARE = WIDTH // DEVICES
 HEAD = 16 * CHIPS
 CHUNK = 24
-READS = [1024] * 4 + [512, 256, 256]
+READS = [1280, 1280, 1280, 768, 512]
 TILE = 256
 BLOCK = 16
 PIECES = [(0, 0, 640), (0, 640, 640), (1, 0, 640), (1, 640, 640)]
-DP_ORDER = [10, 15, 14, 13, 12, 11, 9, 8, 7, 6, 5, 4, 3, 2, 1, 0]
+DP_ORDER = [10, 0, 14, 13, 7, 1, 2, 3, 15, 9, 12, 6, 8, 11, 5, 4]
 CHIP_ORDER = [
     42, 52, 40, 44, 60, 63, 24, 54, 0, 11, 45, 56, 18, 34, 10, 55,
     46, 38, 15, 31, 57, 61, 36, 5, 17, 62, 21, 22, 49, 6, 1, 29,
@@ -95,12 +95,13 @@
 
 
 def chunked(turned_ref, tail_ref, terms):
-    for c in range(CHIPS):
-        tail_ref[c, 0:4, :] = turned_ref[HEAD + 4 * c : HEAD + 4 * c + 4, :]
-    tail_ref[:, 4:8, :] = jnp.broadcast_to(terms[None], (CHIPS, 4, LANES))
+    for n in range(4):
+        tail_ref[pl.ds(n, CHIPS, stride=8), :] = turned_ref[HEAD + CHIPS * n : HEAD + CHIPS * n + CHIPS, :]
+        tail_ref[pl.ds(n + 4, CHIPS, stride=8), :] = jnp.broadcast_to(terms[n : n + 1], (CHIPS, LANES))
     for n in range(CHIPS // 16):
         head = turned_ref[256 * n : 256 * n + 256, :].reshape(16, 16, LANES)
-        yield 16 * n, jnp.concatenate([head, tail_ref[16 * n : 16 * n + 16]], axis=1)
+        tail = tail_ref[128 * n : 128 * n + 128, :].reshape(16, 8, LANES)
+        yield 16 * n, jnp.concatenate([head, tail], axis=1)
 
 
 def other_half_kernel(
@@ -219,13 +220,13 @@
     return pltpu.make_async_copy(stage, out_ref.at[:, :, columns], sem)
 
 
-def half_error(right_ref, left_ref, corrected_ref, out_ref, core, wide_ref, turned_ref, stage_ref, sems, rest_ref=None):
+def half_error(right_ref, left_ref, corrected_ref, out_ref, core, wide_ref, tail_ref, turned_ref, stage_ref, sems, rest_ref=None):
     for n in range(CHIPS // 16):
         block = right_ref[16 * n : 16 * n + 16].astype(F32)
         wide_ref[256 * n : 256 * n + 256, :] = block[:, 0:16].reshape(256, LANES)
-        for c in range(16):
-            start = HEAD + 4 * (16 * n + c)
-            wide_ref[start : start + 4, :] = block[c, 16:20]
+        tail_ref[128 * n : 128 * n + 128, :] = block[:, 16:24].reshape(128, LANES)
+    for n in range(4):
+        wide_ref[HEAD + CHIPS * n : HEAD + CHIPS * n + CHIPS, :] = tail_ref[pl.ds(n, CHIPS, stride=8), :]
     turned_ref[...] = wide_ref[:QUARTER, :].astype(BF16)
 
     copies = []
@@ -320,7 +321,7 @@
     parts = lax.all_to_all(part, "dp", 0, 0, axis_index_groups=[DP_ORDER], tiled=True)
 
     turned = pltpu.VMEM((QUARTER, LANES), F32)
-    tail = pltpu.VMEM((CHIPS, 8, LANES), F32)
+    tail = pltpu.VMEM((CHIPS * 8, LANES), F32)
     chunks = pltpu.VMEM((CHIPS, CHUNK, LANES), BF16)
     half_flops = 2 * MATS * ROWS * HALF * RANK
     for_other, summed, gram_row = call(
@@ -357,6 +358,7 @@
     q_other = lax.ppermute(q_half, "tensor", CORE_PAIRS)
     scratch = [
         pltpu.VMEM((QUARTER + LANES, LANES), F32),
+        tail,
         pltpu.VMEM((QUARTER, LANES), BF16),
         pltpu.VMEM((MATS, ROWS, HALF), BF16),
         pltpu.SemaphoreType.DMA((len(PIECES),)),

time: 69.4 us -> 69.1 us (level)
  no operation moved by 1% of the time
where the time goes in v5:
time: 69.1 us; the launch traced here: 68.9 us
  blocking collectives  48.7 us (70%)
  Pallas kernels  14.8 us (21%)
  starting transfers between devices  4.15 us (6%)
    all_to_all x1, blocking collectives, local(): lax.all_to_all(part, 'dp', 0, 0, axis_index_groups=[DP_ORDER], tiled=True)  18.8 us
    all_to_all x1, blocking collectives, local(): lax.all_to_all(partial_q, BOTH_AXES, 0, 0, axis_index_groups=SAME_CORE, t...  16.3 us
    all_to_all x1, blocking collectives, local(): lax.all_to_all(q_own, BOTH_AXES, 0, 0, axis_index_groups=SAME_CORE, tiled...  13.7 us
    pallas_call x1, Pallas kernels, local(): call(left_kernel, 'left_product', [IN_HBM] * 3, [pltpu.VMEM((MATS, ROWS,...  6.48 us
    pallas_call x1, Pallas kernels, local(): call(other_error_kernel, 'new_error_other', [WHOLE] * 5 + [IN_HBM], [erro...  2.5 us
    ppermute x1, starting transfers between devices, local(): q_other = lax.ppermute(q_half, 'tensor', CORE_PAIRS)  2.38 us
    pallas_call x1, Pallas kernels, local(): call(own_error_kernel, 'new_error_own', [WHOLE] * 4, [error_shape, pltpu....  2.2 us
    ppermute x1, starting transfers between devices, local(): from_other = lax.ppermute(for_other, 'tensor', CORE_PAIRS)  1.78 us
  transfers between devices with their start and end apart: 2, of which 1 were waited for; matrix products, arithmetic and copies ran while one was open for 0% of the time, Pallas kernels for 4%

profile of v5, /device:TPU:1, one launch (start us, length us, event | category | flops | bytes accessed | tf_op | source)
XLA Modules:
  0.0 68.9 jit_solution(16933295753826742935)
XLA Ops:
  0.6 6.5 %left_product.1 = (bf16[2,384,5120]{2,1,0:T(8,128)(2,1)S(1)}, bf16[16,64,384]{2,1,0:T(8,128)(2,1)S(1)}) custom-call(bf16[2,384,5120]{2,1,0:T(8,128)(2,1)} %bitcast.10, bf16[2,384,5120]{2,1,0:T(8,128)(2,1)} %bitcast.11, bf16[2,32,5120]{2,1,0:T(8,128)(2,1)} %bitcast.13), custom_call_target="tpu_custom_call" | custom-call | bytes 4194304 | tf_op jit(solution)/shard_map/left_product/pallas_call | solution.py:308
  7.1 18.8 %all_to_all.15.parts_ref = bf16[16,64,384]{2,1,0:T(8,128)(2,1)S(1)} all-to-all(bf16[16,64,384]{2,1,0:T(8,128)(2,1)S(1)} %get-tuple-element.17), channel_id=1, replica_groups={{80,0,112,104,56,8,16,24,120,72,96,48,64,88,40,32},{81,1,113,105,57,9,1..., dimensions={0} | all-to-all | bytes 1572864 | tf_op jit(solution)/shard_map/all_to_all | solution.py:321
  25.9 1.1 %right_product_other.1 = (bf16[64,24,128]{2,1,0:T(8,128)(2,1)S(1)}, f32[64,384]{1,0:T(8,128)S(1)}, f32[8,128]{1,0:T(8,128)S(1)}) custom-call(bf16[16,64,384]{2,1,0:T(8,128)(2,1)S(1)} %all_to_all.15.parts_ref, bf16[2,384,5120]{2,1,0:T(8,128)(2,1)S(1)} %get-tuple-element.18.corrected_ref), custom_call_target="tpu_custom_call" | custom-call | flops 125829120 | bytes 4194304 | tf_op jit(solution)/shard_map/right_product_other/pallas_call | solution.py:327
  27.0 1.8 %collective-permute-start = (bf16[64,24,128]{2,1,0:T(8,128)(2,1)S(1)}, bf16[64,24,128]{2,1,0:T(8,128)(2,1)S(1)}, u32[]{:S(2)}, u32[]{:S(2)}) collective-permute-start(bf16[64,24,128]{2,1,0:T(8,128)(2,1)S(1)} %get-tuple-element.20), channel_id=1, source_target_pairs={{0,1},{1,0},{2,3},{3,2},{4,5},{5,4},{6,7},{7,6},{8,9},{9,8},{10,11... | collective-permute-start | bytes 1179656 | tf_op jit(solution)/shard_map/ppermute | solution.py:335
  28.8 0.9 %right_product_own.1.own_ref = f32[64,24,128]{2,1,0:T(8,128)S(1)} custom-call(f32[64,384]{1,0:T(8,128)S(1)} %get-tuple-element.19.summed_ref, bf16[2,384,5120]{2,1,0:T(8,128)(2,1)S(1)} %get-tuple-element.18.corrected_ref), custom_call_target="tpu_custom_call" | custom-call | flops 125829120 | bytes 4194304 | tf_op jit(solution)/shard_map/right_product_own/pallas_call | solution.py:336
  29.7 0.5 collective-permute-done.other_ref
  30.1 0.1 pair_sum.1
  30.2 16.3 %all_to_all.16.parts_ref = bf16[64,24,128]{2,1,0:T(8,128)(2,1)S(1)} all-to-all(bf16[64,24,128]{2,1,0:T(8,128)(2,1)S(1)} %pair_sum.1), channel_id=1, replica_groups={{84,104,80,88,120,126,48,108,0,22,90,112,36,68,20,110,92,76,30,62,114,1..., dimensions={0} | all-to-all | bytes 786432 | tf_op jit(solution)/shard_map/all_to_all | solution.py:346
  46.5 1.6 %factor.1 = (bf16[64,24,128]{2,1,0:T(8,128)(2,1)S(1)}, f32[64,384]{1,0:T(8,128)S(1)}, bf16[2,768,128]{2,1,0:T(8,128)(2,1)S(1)}) custom-call(bf16[64,24,128]{2,1,0:T(8,128)(2,1)S(1)} %all_to_all.16.parts_ref, f32[64,384]{1,0:T(8,128)S(1)} %get-tuple-element.19.summed_ref), custom_call_target="tpu_custom_call" | custom-call | bytes 4194304 | tf_op jit(solution)/shard_map/factor/pallas_call | solution.py:348
  48.1 13.7 %all_to_all.17.right_ref = bf16[64,24,128]{2,1,0:T(8,128)(2,1)S(1)} all-to-all(bf16[64,24,128]{2,1,0:T(8,128)(2,1)S(1)} %get-tuple-element.22), channel_id=1, replica_groups={{84,104,80,88,120,126,48,108,0,22,90,112,36,68,20,110,92,76,30,62,114,1..., dimensions={0} | all-to-all | bytes 786432 | tf_op jit(solution)/shard_map/all_to_all | solution.py:356
  61.8 2.4 %collective-permute-start.1 = (bf16[64,24,128]{2,1,0:T(8,128)(2,1)S(1)}, bf16[64,24,128]{2,1,0:T(8,128)(2,1)S(1)}, u32[]{:S(2)}, u32[]{:S(2)}) collective-permute-start(bf16[64,24,128]{2,1,0:T(8,128)(2,1)S(1)} %all_to_all.17.right_ref), channel_id=1, source_target_pairs={{0,1},{1,0},{2,3},{3,2},{4,5},{5,4},{6,7},{7,6},{8,9},{9,8},{10,11... | collective-permute-start | bytes 1179656 | tf_op jit(solution)/shard_map/ppermute | solution.py:358
  64.2 2.2 %new_error_own.1 = (bf16[2,384,5120]{2,1,0:T(8,128)(2,1)}, f32[64,40]{1,0:T(8,128)S(1)}, bf16[2,384,640]{2,1,0:T(8,128)(2,1)S(1)}, f32[64,384]{1,0:T(8,128)}) custom-call(bf16[64,24,128]{2,1,0:T(8,128)(2,1)S(1)} %all_to_all.17.right_ref, bf16[2,768,128]{2,1,0:T(8,128)(2,1)S(1)} %get-tuple-element.23.left_ref, ...), custom_call_target="tpu_custom_call" | custom-call | flops 125829120 | bytes 4194304 | tf_op jit(solution)/shard_map/new_error_own/pallas_call | solution.py:369
  66.4 0.0 collective-permute-done.1.right_ref
  66.4 2.5 %new_error_other.1 = (bf16[2,384,5120]{2,1,0:T(8,128)(2,1)}, f32[64,40]{1,0:T(8,128)}) custom-call(bf16[64,24,128]{2,1,0:T(8,128)(2,1)S(1)} %collective-permute-done.1.right_ref, bf16[2,768,128]{2,1,0:T(8,128)(2,1)S(1)} %get-tuple-element.23.left_ref, bf16[2,384,5120]{2,1,0:T(8,128)(2,1)S(1)} %get-tuple-element.18.corrected_ref, ...), custom_call_target="tpu_custom_call", output_to_operand_aliasing={{0}: (5, {})} | custom-call | flops 125829120 | bytes 4194304 | tf_op jit(solution)/shard_map/new_error_other/pallas_call | solution.py:378
Async XLA Ops:
  27.0 3.1 %collective-permute-start = (bf16[64,24,128]{2,1,0:T(8,128)(2,1)S(1)}, bf16[64,24,128]{2,1,0:T(8,128)(2,1)S(1)}, u32[]{:S(2)}, u32[]{:S(2)}) collective-permute-start(bf16[64,24,128]{2,1,0:T(8,128)(2,1)S(1)} %get-tuple-element.20), channel_id=1, source_target_pairs={{0,1},{1,0},{2,3},{3,2},{4,5},{5,4},{6,7},{7,6},{8,9},{9,8},{10,11... | collective-permute-start | bytes 1179656 | tf_op jit(solution)/shard_map/ppermute | solution.py:335
  61.8 4.6 %collective-permute-start.1 = (bf16[64,24,128]{2,1,0:T(8,128)(2,1)S(1)}, bf16[64,24,128]{2,1,0:T(8,128)(2,1)S(1)}, u32[]{:S(2)}, u32[]{:S(2)}) collective-permute-start(bf16[64,24,128]{2,1,0:T(8,128)(2,1)S(1)} %all_to_all.17.right_ref), channel_id=1, source_target_pairs={{0,1},{1,0},{2,3},{3,2},{4,5},{5,4},{6,7},{7,6},{8,9},{9,8},{10,11... | collective-permute-start | bytes 1179656 | tf_op jit(solution)/shard_map/ppermute | solution.py:358

commit v6 on v5

--- a/solution.py
+++ b/solution.py
@@ -1,3 +1,5 @@
+import functools
+
 import jax
 import jax.numpy as jnp
 from jax import lax
@@ -253,33 +255,43 @@
     return copies, jnp.where(upper, own[BOTH:, :SHARE], own[:BOTH, :SHARE])
 
 
-def own_error_kernel(
-    right_ref, left_ref, corrected_ref, p_ref, out_ref, q_ref, rest_ref, p_out_ref, *scratch
+def own_error_kernel(turn, right_ref, left_ref, corrected_ref, *refs):
+    out_ref, q_ref, rest_ref, *scratch = refs[turn_inputs(turn) :]
+    core = lax.axis_index("tensor") % 2
+
+    @pl.when(core == turn)
+    def _():
+        copies, q_ref[...] = half_error(right_ref, left_ref, corrected_ref, out_ref, core, *scratch, rest_ref)
+        for copy in copies:
+            copy.wait()
+
+
+def turn_inputs(turn):
+    return 1 if turn == 0 else 0
+
+
+def other_error_kernel(
+    right_ref, left_ref, corrected_ref, q_0_ref, rest_0_ref, q_1_ref, rest_1_ref, p_ref, error_ref,
+    out_ref, q_out_ref, p_out_ref, *scratch,
 ):
-    *scratch, p_sem = scratch
+    del error_ref
+    *scratch, q_ref, rest_sem, q_sem, p_sem = scratch
+    core = lax.axis_index("tensor") % 2
     p_copy = pltpu.make_async_copy(p_ref, p_out_ref, p_sem)
     p_copy.start()
-    core = lax.axis_index("tensor") % 2
-    copies, q_ref[...] = half_error(right_ref, left_ref, corrected_ref, out_ref, core, *scratch, rest_ref)
-    for copy in [*copies, p_copy]:
-        copy.wait()
-
-
-def other_error_kernel(
-    right_ref, left_ref, corrected_ref, q_own_ref, rest_ref, error_ref, out_ref, q_out_ref, *scratch
-):
-    del error_ref
-    *scratch, q_ref, rest_sem, q_sem = scratch
-    core = lax.axis_index("tensor") % 2
-    rest_copy = piece_copy(rest_ref, out_ref, core, PIECES[-1], rest_sem)
-    rest_copy.start()
+    rest_copies = [piece_copy(rest, out_ref, core, PIECES[-1], rest_sem) for rest in (rest_0_ref, rest_1_ref)]
+    for turn, copy in enumerate(rest_copies):
+        pl.when(core == turn)(copy.start)
     copies, other = half_error(right_ref, left_ref, corrected_ref, out_ref, 1 - core, *scratch)
     me = lax.axis_index("dp") * TENSOR + lax.axis_index("tensor")
-    q_ref[...] = jnp.where(me // CHIPS == core, q_own_ref[...], other)
+    own = jnp.where(core == 0, q_0_ref[...], q_1_ref[...])
+    q_ref[...] = jnp.where(me // CHIPS == core, own, other)
     q_copy = pltpu.make_async_copy(q_ref, q_out_ref, q_sem)
     q_copy.start()
-    for copy in [rest_copy, *copies, q_copy]:
+    for copy in [*copies, q_copy, p_copy]:
         copy.wait()
+    for turn, copy in enumerate(rest_copies):
+        pl.when(core == turn)(copy.wait)
 
 
 WHOLE = pl.BlockSpec(memory_space=pltpu.VMEM)
@@ -355,7 +367,6 @@
 
     q_half = lax.all_to_all(q_own, BOTH_AXES, 0, 0, axis_index_groups=SAME_CORE, tiled=True)
 
-    q_other = lax.ppermute(q_half, "tensor", CORE_PAIRS)
     scratch = [
         pltpu.VMEM((QUARTER + LANES, LANES), F32),
         tail,
@@ -366,25 +377,37 @@
     error_shape = jax.ShapeDtypeStruct((MATS, ROWS, WIDTH), BF16)
     factor_shape = jax.ShapeDtypeStruct((BOTH, ROWS), F32)
     rest_shape = pltpu.VMEM((MATS, ROWS, PIECES[-1][2]), BF16)
-    new_error, q_factor, rest, p_factor = call(
-        own_error_kernel,
-        "new_error_own",
-        [WHOLE] * 4,
-        [error_shape, pltpu.VMEM((BOTH, SHARE), F32), rest_shape, factor_shape],
-        [IN_HBM, WHOLE, WHOLE, IN_HBM],
-        scratch=[*scratch, pltpu.SemaphoreType.DMA],
+    own_shapes = [error_shape, pltpu.VMEM((BOTH, SHARE), F32), rest_shape]
+    new_error, q_1, rest_1 = call(
+        functools.partial(own_error_kernel, 1),
+        "new_error_own_1",
+        [WHOLE] * 3,
+        own_shapes,
+        [IN_HBM, WHOLE, WHOLE],
+        scratch=scratch,
+    )(q_half, left, corrected)
+    q_half, new_error = lax.optimization_barrier((q_half, new_error))
+    q_other = lax.ppermute(q_half, "tensor", CORE_PAIRS)
+    new_error, q_0, rest_0 = call(
+        functools.partial(own_error_kernel, 0),
+        "new_error_own_0",
+        [WHOLE] * 3 + [IN_HBM],
+        own_shapes,
+        [IN_HBM, WHOLE, WHOLE],
+        scratch=scratch,
         flops=half_flops,
-    )(q_half, left, corrected, p_turned)
-    new_error, q_factor = call(
+        input_output_aliases={3: 0},
+    )(q_half, left, corrected, new_error)
+    new_error, q_factor, p_factor = call(
         other_error_kernel,
         "new_error_other",
-        [WHOLE] * 5 + [IN_HBM],
-        [error_shape, jax.ShapeDtypeStruct((BOTH, SHARE), F32)],
-        [IN_HBM, IN_HBM],
-        scratch=[*scratch, pltpu.VMEM((BOTH, SHARE), F32), pltpu.SemaphoreType.DMA, pltpu.SemaphoreType.DMA],
+        [WHOLE] * 8 + [IN_HBM],
+        [error_shape, jax.ShapeDtypeStruct((BOTH, SHARE), F32), factor_shape],
+        [IN_HBM] * 3,
+        scratch=[*scratch, pltpu.VMEM((BOTH, SHARE), F32)] + [pltpu.SemaphoreType.DMA] * 3,
         flops=half_flops,
-        input_output_aliases={5: 0},
-    )(q_other, left, corrected, q_factor, rest, new_error)
+        input_output_aliases={8: 0},
+    )(q_other, left, corrected, q_0, rest_0, q_1, rest_1, p_turned, new_error)
 
     return (
         new_error[None],

time: 69.1 us -> 68.5 us (level)
  starting transfers between devices: 4.15 us -> 2.13 us
  waiting for transfers between devices: 0.46 us -> 1.87 us
    ppermute x1, starting transfers between devices: 2.38 us -> 0.34 us  [local(): q_other = lax.ppermute(q_half, 'tensor', CORE_PAIRS)]
    ppermute x1, waiting for transfers between devices: 0.01 us -> 1.42 us  [local(): q_other = lax.ppermute(q_half, 'tensor', CORE_PAIRS)]
    pallas_call x2 -> x3, Pallas kernels: 4.7 us -> 4.73 us  [the longest x1 2.54 us: local(): call(other_error_kernel, 'new_error_other', [WHOLE] * 8 + [IN_HBM], [erro...]
  transfers between devices with their start and end apart: 2 -> 2, of which waited for: 1 -> 2; matrix products, arithmetic and copies ran while one was open for 0% -> 0% of each run, Pallas kernels for 4% -> 1%
where the time goes in v6:
time: 68.5 us; the launch traced here: 68.3 us
  blocking collectives  48.7 us (71%)
  Pallas kernels  14.9 us (22%)
  starting transfers between devices  2.13 us (3%)
  waiting for transfers between devices  1.87 us (3%)
    all_to_all x1, blocking collectives, local(): lax.all_to_all(part, 'dp', 0, 0, axis_index_groups=[DP_ORDER], tiled=True)  18.8 us
    all_to_all x1, blocking collectives, local(): lax.all_to_all(partial_q, BOTH_AXES, 0, 0, axis_index_groups=SAME_CORE, t...  16.3 us
    all_to_all x1, blocking collectives, local(): lax.all_to_all(q_own, BOTH_AXES, 0, 0, axis_index_groups=SAME_CORE, tiled...  13.7 us
    pallas_call x1, Pallas kernels, local(): call(left_kernel, 'left_product', [IN_HBM] * 3, [pltpu.VMEM((MATS, ROWS,...  6.48 us
    pallas_call x1, Pallas kernels, local(): call(other_error_kernel, 'new_error_other', [WHOLE] * 8 + [IN_HBM], [erro...  2.54 us
    pallas_call x1, Pallas kernels, local(): call(functools.partial(own_error_kernel, 1), 'new_error_own_1', [WHOLE] *...  2.15 us
    ppermute x1, starting transfers between devices, local(): from_other = lax.ppermute(for_other, 'tensor', CORE_PAIRS)  1.79 us
    pallas_call x1, Pallas kernels, local(): call(factor_kernel, 'factor', [WHOLE] * 2, [chunks, pltpu.VMEM((BOTH, ROW...  1.57 us
  transfers between devices with their start and end apart: 2, of which 2 were waited for; matrix products, arithmetic and copies ran while one was open for 0% of the time, Pallas kernels for 1%

profile of v6, /device:TPU:1, one launch (start us, length us, event | category | flops | bytes accessed | tf_op | source)
XLA Modules:
  0.0 68.3 jit_solution(7418680520571390307)
XLA Ops:
  0.6 6.5 %left_product.1 = (bf16[2,384,5120]{2,1,0:T(8,128)(2,1)S(1)}, bf16[16,64,384]{2,1,0:T(8,128)(2,1)S(1)}) custom-call(bf16[2,384,5120]{2,1,0:T(8,128)(2,1)} %bitcast.11, bf16[2,384,5120]{2,1,0:T(8,128)(2,1)} %bitcast.12, bf16[2,32,5120]{2,1,0:T(8,128)(2,1)} %bitcast.13), custom_call_target="tpu_custom_call" | custom-call | bytes 4194304 | tf_op jit(solution)/shard_map/left_product/pallas_call | solution.py:320
  7.1 18.8 %all_to_all.15.parts_ref = bf16[16,64,384]{2,1,0:T(8,128)(2,1)S(1)} all-to-all(bf16[16,64,384]{2,1,0:T(8,128)(2,1)S(1)} %get-tuple-element.22), channel_id=1, replica_groups={{80,0,112,104,56,8,16,24,120,72,96,48,64,88,40,32},{81,1,113,105,57,9,1..., dimensions={0} | all-to-all | bytes 1572864 | tf_op jit(solution)/shard_map/all_to_all | solution.py:333
  25.9 1.1 %right_product_other.1 = (bf16[64,24,128]{2,1,0:T(8,128)(2,1)S(1)}, f32[64,384]{1,0:T(8,128)S(1)}, f32[8,128]{1,0:T(8,128)S(1)}) custom-call(bf16[16,64,384]{2,1,0:T(8,128)(2,1)S(1)} %all_to_all.15.parts_ref, bf16[2,384,5120]{2,1,0:T(8,128)(2,1)S(1)} %get-tuple-element.23.corrected_ref), custom_call_target="tpu_custom_call" | custom-call | flops 125829120 | bytes 4194304 | tf_op jit(solution)/shard_map/right_product_other/pallas_call | solution.py:339
  27.0 1.8 %collective-permute-start = (bf16[64,24,128]{2,1,0:T(8,128)(2,1)S(1)}, bf16[64,24,128]{2,1,0:T(8,128)(2,1)S(1)}, u32[]{:S(2)}, u32[]{:S(2)}) collective-permute-start(bf16[64,24,128]{2,1,0:T(8,128)(2,1)S(1)} %get-tuple-element.25), channel_id=1, source_target_pairs={{0,1},{1,0},{2,3},{3,2},{4,5},{5,4},{6,7},{7,6},{8,9},{9,8},{10,11... | collective-permute-start | bytes 1179656 | tf_op jit(solution)/shard_map/ppermute | solution.py:347
  28.8 0.9 %right_product_own.1.own_ref = f32[64,24,128]{2,1,0:T(8,128)S(1)} custom-call(f32[64,384]{1,0:T(8,128)S(1)} %get-tuple-element.24.summed_ref, bf16[2,384,5120]{2,1,0:T(8,128)(2,1)S(1)} %get-tuple-element.23.corrected_ref), custom_call_target="tpu_custom_call" | custom-call | flops 125829120 | bytes 4194304 | tf_op jit(solution)/shard_map/right_product_own/pallas_call | solution.py:348
  29.7 0.5 collective-permute-done.other_ref
  30.2 0.1 pair_sum.1
  30.3 16.3 %all_to_all.16.parts_ref = bf16[64,24,128]{2,1,0:T(8,128)(2,1)S(1)} all-to-all(bf16[64,24,128]{2,1,0:T(8,128)(2,1)S(1)} %pair_sum.1), channel_id=1, replica_groups={{84,104,80,88,120,126,48,108,0,22,90,112,36,68,20,110,92,76,30,62,114,1..., dimensions={0} | all-to-all | bytes 786432 | tf_op jit(solution)/shard_map/all_to_all | solution.py:358
  46.5 1.6 %factor.1 = (bf16[64,24,128]{2,1,0:T(8,128)(2,1)S(1)}, f32[64,384]{1,0:T(8,128)S(1)}, bf16[2,768,128]{2,1,0:T(8,128)(2,1)S(1)}) custom-call(bf16[64,24,128]{2,1,0:T(8,128)(2,1)S(1)} %all_to_all.16.parts_ref, f32[64,384]{1,0:T(8,128)S(1)} %get-tuple-element.24.summed_ref), custom_call_target="tpu_custom_call" | custom-call | bytes 4194304 | tf_op jit(solution)/shard_map/factor/pallas_call | solution.py:360
  48.1 13.7 %all_to_all.17.right_ref = bf16[64,24,128]{2,1,0:T(8,128)(2,1)S(1)} all-to-all(bf16[64,24,128]{2,1,0:T(8,128)(2,1)S(1)} %get-tuple-element.27), channel_id=1, replica_groups={{84,104,80,88,120,126,48,108,0,22,90,112,36,68,20,110,92,76,30,62,114,1..., dimensions={0} | all-to-all | bytes 786432 | tf_op jit(solution)/shard_map/all_to_all | solution.py:368
  61.8 2.2 %new_error_own_1.1 = (bf16[2,384,5120]{2,1,0:T(8,128)(2,1)}, f32[64,40]{1,0:T(8,128)S(1)}, bf16[2,384,640]{2,1,0:T(8,128)(2,1)S(1)}) custom-call(bf16[64,24,128]{2,1,0:T(8,128)(2,1)S(1)} %all_to_all.17.right_ref, bf16[2,768,128]{2,1,0:T(8,128)(2,1)S(1)} %get-tuple-element.28.left_ref, bf16[2,384,5120]{2,1,0:T(8,128)(2,1)S(1)} %get-tuple-element.23.corrected_ref), custom_call_target="tpu_custom_call" | custom-call | bytes 4194304 | tf_op jit(solution)/shard_map/new_error_own_1/pallas_call | solution.py:381
  64.0 0.3 collective-permute-start.1
  64.3 1.4 %collective-permute-done.1.right_ref = bf16[64,24,128]{2,1,0:T(8,128)(2,1)S(1)} collective-permute-done((bf16[64,24,128]{2,1,0:T(8,128)(2,1)S(1)}, bf16[64,24,128]{2,1,0:T(8,128)(2,1)S(1)}, u32[]{:S(2)}, u32[]{:S(2)}) %collective-permute-start.1) | collective-permute-done | bytes 393248 | tf_op jit(solution)/shard_map/ppermute | solution.py:390
  65.8 2.5 %new_error_other.1 = (bf16[2,384,5120]{2,1,0:T(8,128)(2,1)}, f32[64,40]{1,0:T(8,128)}, f32[64,384]{1,0:T(8,128)}) custom-call(bf16[64,24,128]{2,1,0:T(8,128)(2,1)S(1)} %collective-permute-done.1.right_ref, bf16[2,768,128]{2,1,0:T(8,128)(2,1)S(1)} %get-tuple-element.28.left_ref, ...), custom_call_target="tpu_custom_call", output_to_operand_aliasing={{0}: (8, {})} | custom-call | flops 125829120 | bytes 4194304 | tf_op jit(solution)/shard_map/new_error_other/pallas_call | solution.py:401
  (1 shorter events, 0.0 us)
Async XLA Ops:
  27.0 3.1 %collective-permute-start = (bf16[64,24,128]{2,1,0:T(8,128)(2,1)S(1)}, bf16[64,24,128]{2,1,0:T(8,128)(2,1)S(1)}, u32[]{:S(2)}, u32[]{:S(2)}) collective-permute-start(bf16[64,24,128]{2,1,0:T(8,128)(2,1)S(1)} %get-tuple-element.25), channel_id=1, source_target_pairs={{0,1},{1,0},{2,3},{3,2},{4,5},{5,4},{6,7},{7,6},{8,9},{9,8},{10,11... | collective-permute-start | bytes 1179656 | tf_op jit(solution)/shard_map/ppermute | solution.py:347
  64.0 1.8 %collective-permute-start.1 = (bf16[64,24,128]{2,1,0:T(8,128)(2,1)S(1)}, bf16[64,24,128]{2,1,0:T(8,128)(2,1)S(1)}, u32[]{:S(2)}, u32[]{:S(2)}) collective-permute-start(bf16[64,24,128]{2,1,0:T(8,128)(2,1)S(1)} %all_to_all.17.right_ref), channel_id=1, source_target_pairs={{0,1},{1,0},{2,3},{3,2},{4,5},{5,4},{6,7},{7,6},{8,9},{9,8},{10,11... | collective-permute-start | bytes 1179656 | tf_op jit(solution)/shard_map/ppermute | solution.py:390

commit v7 on v6

--- a/solution.py
+++ b/solution.py
@@ -29,7 +29,7 @@
 TILE = 256
 BLOCK = 16
 PIECES = [(0, 0, 640), (0, 640, 640), (1, 0, 640), (1, 640, 640)]
-DP_ORDER = [10, 0, 14, 13, 7, 1, 2, 3, 15, 9, 12, 6, 8, 11, 5, 4]
+DP_ORDER = [10, 14, 7, 5, 2, 6, 15, 4, 0, 3, 8, 11, 1, 13, 9, 12]
 CHIP_ORDER = [
     42, 52, 40, 44, 60, 63, 24, 54, 0, 11, 45, 56, 18, 34, 10, 55,
     46, 38, 15, 31, 57, 61, 36, 5, 17, 62, 21, 22, 49, 6, 1, 29,

time: 68.5 us -> 68.1 us (level)
    all_to_all x1, blocking collectives: 16.3 us -> 15.4 us  [local(): lax.all_to_all(partial_q, BOTH_AXES, 0, 0, axis_index_groups=SAME_CORE, t...]
where the time goes in v7:
time: 68.1 us; the launch traced here: 67.9 us
  blocking collectives  48.2 us (71%)
  Pallas kernels  14.9 us (22%)
  starting transfers between devices  2.33 us (3%)
  waiting for transfers between devices  1.87 us (3%)
    all_to_all x1, blocking collectives, local(): lax.all_to_all(part, 'dp', 0, 0, axis_index_groups=[DP_ORDER], tiled=True)  18.9 us
    all_to_all x1, blocking collectives, local(): lax.all_to_all(partial_q, BOTH_AXES, 0, 0, axis_index_groups=SAME_CORE, t...  15.4 us
    all_to_all x1, blocking collectives, local(): lax.all_to_all(q_own, BOTH_AXES, 0, 0, axis_index_groups=SAME_CORE, tiled...  13.9 us
    pallas_call x1, Pallas kernels, local(): call(left_kernel, 'left_product', [IN_HBM] * 3, [pltpu.VMEM((MATS, ROWS,...  6.48 us
    pallas_call x1, Pallas kernels, local(): call(other_error_kernel, 'new_error_other', [WHOLE] * 8 + [IN_HBM], [erro...  2.54 us
    pallas_call x1, Pallas kernels, local(): call(functools.partial(own_error_kernel, 1), 'new_error_own_1', [WHOLE] *...  2.15 us
    ppermute x1, starting transfers between devices, local(): from_other = lax.ppermute(for_other, 'tensor', CORE_PAIRS)  1.99 us
    pallas_call x1, Pallas kernels, local(): call(factor_kernel, 'factor', [WHOLE] * 2, [chunks, pltpu.VMEM((BOTH, ROW...  1.57 us
  transfers between devices with their start and end apart: 2, of which 2 were waited for; matrix products, arithmetic and copies ran while one was open for 0% of the time, Pallas kernels for 1%

profile of v7, /device:TPU:1, one launch (start us, length us, event | category | flops | bytes accessed | tf_op | source)
XLA Modules:
  0.0 67.9 jit_solution(11180189280404439026)
XLA Ops:
  0.6 6.5 %left_product.1 = (bf16[2,384,5120]{2,1,0:T(8,128)(2,1)S(1)}, bf16[16,64,384]{2,1,0:T(8,128)(2,1)S(1)}) custom-call(bf16[2,384,5120]{2,1,0:T(8,128)(2,1)} %bitcast.11, bf16[2,384,5120]{2,1,0:T(8,128)(2,1)} %bitcast.12, bf16[2,32,5120]{2,1,0:T(8,128)(2,1)} %bitcast.13), custom_call_target="tpu_custom_call" | custom-call | bytes 4194304 | tf_op jit(solution)/shard_map/left_product/pallas_call | solution.py:320
  7.1 18.9 %all_to_all.15.parts_ref = bf16[16,64,384]{2,1,0:T(8,128)(2,1)S(1)} all-to-all(bf16[16,64,384]{2,1,0:T(8,128)(2,1)S(1)} %get-tuple-element.22), channel_id=1, replica_groups={{80,112,56,40,16,48,120,32,0,24,64,88,8,104,72,96},{81,113,57,41,17,49,..., dimensions={0} | all-to-all | bytes 1572864 | tf_op jit(solution)/shard_map/all_to_all | solution.py:333
  26.0 1.1 %right_product_other.1 = (bf16[64,24,128]{2,1,0:T(8,128)(2,1)S(1)}, f32[64,384]{1,0:T(8,128)S(1)}, f32[8,128]{1,0:T(8,128)S(1)}) custom-call(bf16[16,64,384]{2,1,0:T(8,128)(2,1)S(1)} %all_to_all.15.parts_ref, bf16[2,384,5120]{2,1,0:T(8,128)(2,1)S(1)} %get-tuple-element.23.corrected_ref), custom_call_target="tpu_custom_call" | custom-call | flops 125829120 | bytes 4194304 | tf_op jit(solution)/shard_map/right_product_other/pallas_call | solution.py:339
  27.1 2.0 %collective-permute-start = (bf16[64,24,128]{2,1,0:T(8,128)(2,1)S(1)}, bf16[64,24,128]{2,1,0:T(8,128)(2,1)S(1)}, u32[]{:S(2)}, u32[]{:S(2)}) collective-permute-start(bf16[64,24,128]{2,1,0:T(8,128)(2,1)S(1)} %get-tuple-element.25), channel_id=1, source_target_pairs={{0,1},{1,0},{2,3},{3,2},{4,5},{5,4},{6,7},{7,6},{8,9},{9,8},{10,11... | collective-permute-start | bytes 1179656 | tf_op jit(solution)/shard_map/ppermute | solution.py:347
  29.1 0.9 %right_product_own.1.own_ref = f32[64,24,128]{2,1,0:T(8,128)S(1)} custom-call(f32[64,384]{1,0:T(8,128)S(1)} %get-tuple-element.24.summed_ref, bf16[2,384,5120]{2,1,0:T(8,128)(2,1)S(1)} %get-tuple-element.23.corrected_ref), custom_call_target="tpu_custom_call" | custom-call | flops 125829120 | bytes 4194304 | tf_op jit(solution)/shard_map/right_product_own/pallas_call | solution.py:348
  30.0 0.5 collective-permute-done.other_ref
  30.4 0.1 pair_sum.1
  30.5 15.4 %all_to_all.16.parts_ref = bf16[64,24,128]{2,1,0:T(8,128)(2,1)S(1)} all-to-all(bf16[64,24,128]{2,1,0:T(8,128)(2,1)S(1)} %pair_sum.1), channel_id=1, replica_groups={{84,104,80,88,120,126,48,108,0,22,90,112,36,68,20,110,92,76,30,62,114,1..., dimensions={0} | all-to-all | bytes 786432 | tf_op jit(solution)/shard_map/all_to_all | solution.py:358
  46.0 1.6 %factor.1 = (bf16[64,24,128]{2,1,0:T(8,128)(2,1)S(1)}, f32[64,384]{1,0:T(8,128)S(1)}, bf16[2,768,128]{2,1,0:T(8,128)(2,1)S(1)}) custom-call(bf16[64,24,128]{2,1,0:T(8,128)(2,1)S(1)} %all_to_all.16.parts_ref, f32[64,384]{1,0:T(8,128)S(1)} %get-tuple-element.24.summed_ref), custom_call_target="tpu_custom_call" | custom-call | bytes 4194304 | tf_op jit(solution)/shard_map/factor/pallas_call | solution.py:360
  47.5 13.9 %all_to_all.17.right_ref = bf16[64,24,128]{2,1,0:T(8,128)(2,1)S(1)} all-to-all(bf16[64,24,128]{2,1,0:T(8,128)(2,1)S(1)} %get-tuple-element.27), channel_id=1, replica_groups={{84,104,80,88,120,126,48,108,0,22,90,112,36,68,20,110,92,76,30,62,114,1..., dimensions={0} | all-to-all | bytes 786432 | tf_op jit(solution)/shard_map/all_to_all | solution.py:368
  61.4 2.2 %new_error_own_1.1 = (bf16[2,384,5120]{2,1,0:T(8,128)(2,1)}, f32[64,40]{1,0:T(8,128)S(1)}, bf16[2,384,640]{2,1,0:T(8,128)(2,1)S(1)}) custom-call(bf16[64,24,128]{2,1,0:T(8,128)(2,1)S(1)} %all_to_all.17.right_ref, bf16[2,768,128]{2,1,0:T(8,128)(2,1)S(1)} %get-tuple-element.28.left_ref, bf16[2,384,5120]{2,1,0:T(8,128)(2,1)S(1)} %get-tuple-element.23.corrected_ref), custom_call_target="tpu_custom_call" | custom-call | bytes 4194304 | tf_op jit(solution)/shard_map/new_error_own_1/pallas_call | solution.py:381
  63.6 0.3 collective-permute-start.1
  64.0 1.4 %collective-permute-done.1.right_ref = bf16[64,24,128]{2,1,0:T(8,128)(2,1)S(1)} collective-permute-done((bf16[64,24,128]{2,1,0:T(8,128)(2,1)S(1)}, bf16[64,24,128]{2,1,0:T(8,128)(2,1)S(1)}, u32[]{:S(2)}, u32[]{:S(2)}) %collective-permute-start.1) | collective-permute-done | bytes 393248 | tf_op jit(solution)/shard_map/ppermute | solution.py:390
  65.4 2.5 %new_error_other.1 = (bf16[2,384,5120]{2,1,0:T(8,128)(2,1)}, f32[64,40]{1,0:T(8,128)}, f32[64,384]{1,0:T(8,128)}) custom-call(bf16[64,24,128]{2,1,0:T(8,128)(2,1)S(1)} %collective-permute-done.1.right_ref, bf16[2,768,128]{2,1,0:T(8,128)(2,1)S(1)} %get-tuple-element.28.left_ref, ...), custom_call_target="tpu_custom_call", output_to_operand_aliasing={{0}: (8, {})} | custom-call | flops 125829120 | bytes 4194304 | tf_op jit(solution)/shard_map/new_error_other/pallas_call | solution.py:401
  (1 shorter events, 0.0 us)
Async XLA Ops:
  27.1 3.3 %collective-permute-start = (bf16[64,24,128]{2,1,0:T(8,128)(2,1)S(1)}, bf16[64,24,128]{2,1,0:T(8,128)(2,1)S(1)}, u32[]{:S(2)}, u32[]{:S(2)}) collective-permute-start(bf16[64,24,128]{2,1,0:T(8,128)(2,1)S(1)} %get-tuple-element.25), channel_id=1, source_target_pairs={{0,1},{1,0},{2,3},{3,2},{4,5},{5,4},{6,7},{7,6},{8,9},{9,8},{10,11... | collective-permute-start | bytes 1179656 | tf_op jit(solution)/shard_map/ppermute | solution.py:347
  63.6 1.8 %collective-permute-start.1 = (bf16[64,24,128]{2,1,0:T(8,128)(2,1)S(1)}, bf16[64,24,128]{2,1,0:T(8,128)(2,1)S(1)}, u32[]{:S(2)}, u32[]{:S(2)}) collective-permute-start(bf16[64,24,128]{2,1,0:T(8,128)(2,1)S(1)} %all_to_all.17.right_ref), channel_id=1, source_target_pairs={{0,1},{1,0},{2,3},{3,2},{4,5},{5,4},{6,7},{7,6},{8,9},{9,8},{10,11... | collective-permute-start | bytes 1179656 | tf_op jit(solution)/shard_map/ppermute | solution.py:390
